TPU v7x, 512 devices: a whole 4x4x16 slice. The times are simulated.
512 devices in a mesh: step: 8 (over y, core), node: 2 (over x_lo), space: 32 (over x_hi, z).
Axes of the slice: x: 4 (x_hi: 2, x_lo: 2; x = x_hi * 2 + x_lo), y: 4, z: 16, core: 2. Of those that a mesh axis runs over, the one named last changes fastest.
Arguments:
- iterate: float32 [16, 4, 64, 32, 256], P('step', 'node', 'space'), may hold values from -2.5 to 2.5
- initial_value: float32 [64, 32, 256], P('space'), may hold values from -2.5 to 2.5
- alpha_power: int32 [1], replicated, may hold values from 8 to 72
- node_mix: float32 [2, 16, 4, 4], P(None, 'step', 'node'), may hold values from -0.4 to 1.4
- node_back: float32 [2, 16, 4, 4], P(None, 'step', 'node'), may hold values from -0.4 to 1.4
- shifts: float32 [2, 16, 4], P(None, 'step', 'node'), may hold values from -0.4 to 0.8, as said below
Outputs:
- updated: float32 [16, 4, 64, 32, 256], P('step', 'node', 'space')
- new_residual: float32 [16, 4, 64, 32, 256], P('step', 'node', 'space')
Inputs may be any that keep to these rules, and one draw needn't show every extreme that they name: shifts[0] lies in 0.2 to 0.8, shifts[1] in -0.4 to 0.4.
All inputs are finite; a program needn't handle non-finite values.
Results may differ from a plain program's by a relative error of at most 0.0003.
Values sent between devices are 32-bit elements; how exact they have to be, the bound alone decides.
A program may use at most 64 MiB of HBM per device.

v0:
```python
import math

import jax
import jax.numpy as jnp
from jax import lax
from jax.sharding import PartitionSpec as P

STEPS = 16
NODES = 4
SWEEPS = 8


DIFFUSION = 0.5
REACTION = 1.0


def padded_2(array, sides, width):
    for axis, dim in sides:
        peers, length = (lax.axis_size(axis), array.shape[dim])
        up = [(i, (i + 1) % peers) for i in range(peers - 1)]
        down = [(j, i) for i, j in up]
        last = lax.slice_in_dim(array, length - width, length, axis=dim)
        leading = lax.slice_in_dim(array, 0, width, axis=dim)
        before = lax.ppermute(last, axis, up)
        after = lax.ppermute(leading, axis, down)
        array = jnp.concatenate([before, array, after], axis=dim)
    return array


def spread(value, axis, source):
    kept = jnp.where(lax.axis_index(axis) == source, value, 0).astype(value.dtype)
    return lax.psum(kept, axis)


def shifted(block, axis, distance):
    devices = range(lax.axis_size(axis))
    route = [(i - distance, i) for i in devices if i - distance in devices]
    return lax.ppermute(block, axis, route)


def legendre_pair(degree, point):
    previous_term, current_term = (1.0, point)
    for degree_now in range(1, degree):
        previous_term, current_term = (
            current_term,
            ((2 * degree_now + 1) * point * current_term - degree_now * previous_term)
            / (degree_now + 1),
        )
    return (current_term, previous_term)


def radau_value(count, point):
    high_term, low_term = legendre_pair(count, point)
    return high_term - low_term


def radau_points(count):
    roots_found = []
    samples = 4000
    for sample_index in range(samples):
        left_end = -1.0 + 2.0 * sample_index / samples
        right_end = -1.0 + 2.0 * (sample_index + 1) / samples
        if radau_value(count, left_end) * radau_value(count, right_end) < 0.0:
            for halving in range(200):
                middle = 0.5 * (left_end + right_end)
                if radau_value(count, left_end) * radau_value(count, middle) <= 0.0:
                    right_end = middle
                else:
                    left_end = middle
            roots_found.append(0.5 * (left_end + right_end))
    roots_found.append(1.0)
    return [(root_value + 1.0) / 2.0 for root_value in roots_found]


def collocation_matrix(node_count):
    points = radau_points(node_count)
    node_table = [[0.0] * node_count for row_number in range(node_count)]
    for column in range(node_count):
        coeffs = [1.0]
        for another in range(node_count):
            if another != column:
                spacing = points[column] - points[another]
                raised = [0.0] + coeffs
                lowered = [entry * points[another] for entry in coeffs] + [0.0]
                coeffs = [
                    (first_entry - second_entry) / spacing
                    for first_entry, second_entry in zip(raised, lowered)
                ]
        integral = [0.0] + [
            entry / (exponent_index + 1) for exponent_index, entry in enumerate(coeffs)
        ]
        for row_number in range(node_count):
            running = 0.0
            for exponent_index in range(len(integral) - 1, -1, -1):
                running = running * points[row_number] + integral[exponent_index]
            node_table[row_number][column] = running
    return node_table


def fourier_tables(length):
    indices = jnp.arange(length, dtype=jnp.int32)
    product = indices[:, None] * indices[None, :] % length
    angles = product.astype(jnp.float32) * (2.0 * math.pi / length)
    return (jnp.cos(angles), jnp.sin(angles))


def neighbours(padded):
    middle = padded[..., 1:-1, :, :]
    running = padded[..., 2:, :, :] + padded[..., :-2, :, :]
    widths = [(0, 0)] * (middle.ndim - 2) + [(1, 1), (0, 0)]
    across = jnp.pad(middle, widths)
    running = running + across[..., 2:, :] + across[..., :-2, :]
    widths = [(0, 0)] * (middle.ndim - 1) + [(1, 1)]
    across = jnp.pad(middle, widths)
    return running + across[..., 2:] + across[..., :-2]


def shift_terms(shifts):
    shift_re = shifts[0][:, :, None, None, None]
    shift_im = shifts[1][:, :, None, None, None]
    coef_re = DIFFUSION * shift_re
    coef_im = DIFFUSION * shift_im
    diag_re = 1.0 + (6.0 * DIFFUSION - REACTION) * shift_re
    diag_im = (6.0 * DIFFUSION - REACTION) * shift_im
    magnitude = diag_re * diag_re + diag_im * diag_im
    return (coef_re, coef_im, diag_re / magnitude, -diag_im / magnitude)


def scale_rows(source, shift_coefs):
    inv_re, inv_im = (shift_coefs[2], shift_coefs[3])
    return jnp.stack(
        [source[0] * inv_re - source[1] * inv_im, source[0] * inv_im + source[1] * inv_re]
    )


def sweep_rows(padded, source, shift_coefs):
    coef_re, coef_im, inv_re, inv_im = shift_coefs
    beside_all = neighbours(padded)
    target_re = source[0] + coef_re * beside_all[0] - coef_im * beside_all[1]
    target_im = source[1] + coef_re * beside_all[1] + coef_im * beside_all[0]
    return jnp.stack(
        [target_re * inv_re - target_im * inv_im, target_re * inv_im + target_im * inv_re]
    )


def reaction_residual(grid_field, initial_value, node_rows):
    local_nodes = grid_field.shape[1]
    padded = padded_2(grid_field, (("space", 2),), 1)
    forcing = DIFFUSION * (neighbours(padded) - 6.0 * grid_field) + REACTION * (
        grid_field - grid_field * grid_field * grid_field
    )
    shard_piece = lax.all_gather(forcing, "node", axis=1, tiled=True)
    columns = lax.slice_in_dim(node_rows, 0, shard_piece.shape[1], axis=1)
    mixed_terms = jnp.zeros_like(grid_field) + jnp.einsum(
        "mj,sjzxy->smzxy", columns, shard_piece, precision=lax.Precision.HIGHEST
    )
    final_node = spread(grid_field[:, local_nodes - 1], "node", lax.axis_size("node") - 1)
    before = shifted(final_node[-1:], "step", 1)
    opening = jnp.where(lax.axis_index("step") == 0, initial_value[None], before)
    previous = jnp.concatenate([opening, final_node[:-1]], 0)
    return previous[:, None] + mixed_terms - grid_field


def complex_mix(matrix_pair, real_part, imag_part, form):
    high = lax.Precision.HIGHEST
    out_re = jnp.einsum(form, matrix_pair[0], real_part, precision=high) - jnp.einsum(
        form, matrix_pair[1], imag_part, precision=high
    )
    out_im = jnp.einsum(form, matrix_pair[0], imag_part, precision=high) + jnp.einsum(
        form, matrix_pair[1], real_part, precision=high
    )
    return (out_re, out_im)


def on_device(iterate, initial_value, alpha_power, node_mix, node_back, shifts):
    high = lax.Precision.HIGHEST
    local_steps, local_nodes = (iterate.shape[0], iterate.shape[1])
    node_table = jnp.asarray(collocation_matrix(NODES), jnp.float32)
    node_rows = lax.dynamic_slice_in_dim(
        node_table, lax.axis_index("node") * local_nodes, local_nodes, 0
    )
    residual = reaction_residual(iterate, initial_value, node_rows)
    exponent = alpha_power[0].astype(jnp.float32) / 16.0
    step_first = lax.axis_index("step") * local_steps
    local_values = (step_first + jnp.arange(local_steps, dtype=jnp.int32)).astype(jnp.float32)
    scaled = residual * jnp.exp2(-exponent * local_values / STEPS)[:, None, None, None, None]
    cosine, sine_table = fourier_tables(STEPS)
    gathered = lax.all_to_all(scaled, "step", split_axis=3, concat_axis=0, tiled=True)
    whole_re = jnp.einsum("kn,nmzxy->kmzxy", cosine, gathered, precision=high)
    whole_im = -jnp.einsum("kn,nmzxy->kmzxy", sine_table, gathered, precision=high)
    spec_re, spec_im = (
        lax.all_to_all(whole_re, "step", split_axis=0, concat_axis=3, tiled=True),
        lax.all_to_all(whole_im, "step", split_axis=0, concat_axis=3, tiled=True),
    )
    empty_field = jnp.zeros_like(spec_re)
    pieces = (
        lax.all_gather(spec_re, "node", axis=1, tiled=True),
        lax.all_gather(spec_im, "node", axis=1, tiled=True),
    )
    columns = lax.slice_in_dim(node_mix, 0, pieces[0].shape[1], axis=3)
    part_re, part_im = complex_mix(columns, pieces[0], pieces[1], "smj,sjzxy->smzxy")
    source_re = empty_field + part_re
    source_im = empty_field + part_im
    source = jnp.stack([source_re, source_im])
    shift_coefs = shift_terms(shifts)
    solved = scale_rows(source, shift_coefs)
    for sweep_index in range(SWEEPS - 1):
        padded = padded_2(solved, (("space", 3),), 1)
        solved = sweep_rows(padded, source, shift_coefs)
    shard_piece = lax.all_gather(solved, "node", axis=2, tiled=True)
    columns = lax.slice_in_dim(node_back, 0, shard_piece.shape[2], axis=3)
    part_re, part_im = complex_mix(columns, shard_piece[0], shard_piece[1], "smj,sjzxy->smzxy")
    backed = jnp.zeros_like(solved) + jnp.stack([part_re, part_im])
    freq_re, freq_im = (
        lax.all_to_all(backed[0], "step", split_axis=3, concat_axis=0, tiled=True),
        lax.all_to_all(backed[1], "step", split_axis=3, concat_axis=0, tiled=True),
    )
    step_values = jnp.arange(STEPS, dtype=jnp.int32).astype(jnp.float32)
    back_scale = (jnp.exp2(exponent * step_values / STEPS) / STEPS)[:, None, None, None, None]
    correction = jnp.einsum("nk,kmzxy->nmzxy", cosine, freq_re, precision=high) - jnp.einsum(
        "nk,kmzxy->nmzxy", sine_table, freq_im, precision=high
    )
    correction = lax.all_to_all(
        correction * back_scale, "step", split_axis=0, concat_axis=3, tiled=True
    )
    updated = iterate + correction
    return (updated, reaction_residual(updated, initial_value, node_rows))


def solution(mesh):
    in_specs = (
        P("step", "node", "space", None, None),
        P("space", None, None),
        P(),
        P(None, "step", "node", None),
        P(None, "step", "node", None),
        P(None, "step", "node"),
    )
    out_specs = (P("step", "node", "space", None, None), P("step", "node", "space", None, None))
    return jax.shard_map(
        on_device, mesh=mesh, in_specs=in_specs, out_specs=out_specs, check_vma=False
    )
```

profile of v0, /device:TPU:1, one launch (start us, length us, event | category | flops | bytes accessed | tf_op | source)
XLA Modules:
  0.0 374.9 jit_solution(9979430576541832421)
XLA Ops:
  10.2 5.0 %collective-permute-start.2 = (f32[2,2,1,32,256]{4,3,2,1,0:T(8,128)S(1)}, f32[2,2,1,32,256]{4,3,2,1,0:T(8,128)S(1)}, u32[]{:S(2)}, u32[]{:S(2)}) collective-permute-start(f32[2,2,1,32,256]{4,3,2,1,0:T(8,128)S(1)} %get-tuple-element.48), channel_id=1, source_target_pairs={{0,1},{1,2},{2,3},{3,4},{4,5},{5,6},{6,7},{7,8},{8,9},{9,10},{10,1... | collective-permute-start | bytes 393224 | tf_op jit(solution)/shard_map/ppermute | solution.py:24
  15.9 43.9 %all-reduce.21.cloned.1.call-done = f32[2,2,32,256]{3,2,1,0:T(8,128)} async-done(((f32[2,2,32,256]{3,2,1,0:T(8,128)}), f32[2,2,32,256]{3,2,1,0:T(8,128)}) %all-reduce.21.cloned.1.call-update) | async-done | bytes 131088 | tf_op jit(solution)/shard_map/psum | solution.py:32
  65.1 7.5 %all_gather.15 = f32[2,4,2,32,256]{4,3,2,0,1:T(8,128)S(1)} all-gather(f32[2,2,2,32,256]{4,3,2,0,1:T(8,128)S(1)} %copy.75), channel_id=1, replica_groups=mesh['step'=8,'node'=2,'space'=32] {'node'}, dimensions={1}, use_global_device_ids=true | all-gather | bytes 786432 | tf_op jit(solution)/shard_map/all_gather | solution.py:152
  74.2 11.6 %all_to_all.108 = f32[2,2,2,32,256]{4,1,2,0,3:T(2,128)S(1)} all-to-all(f32[2,2,2,32,256]{4,1,2,0,3:T(2,128)S(1)} %copy.78), channel_id=1, replica_groups=mesh['step'=8,'node'=2,'space'=32] {'step'}, dimensions={3} | all-to-all | bytes 524288 | tf_op jit(solution)/shard_map/all_to_all | solution.py:188
  87.4 4.4 %all-to-all-start.2 = ((f32[16,2,2,4,256]{4,3,2,1,0:T(4,128)}), f32[16,2,2,4,256]{4,3,2,1,0:T(4,128)S(1)}, u32[]{:S(2)}, u32[]{:S(2)}) async-start(f32[16,2,2,4,256]{4,3,2,1,0:T(4,128)} %copy.83), calls=%async_computation.2 | async-start | bytes 524288 | tf_op jit(solution)/shard_map/all_to_all | solution.py:193
  93.1 5.2 %all-to-all-done.2 = f32[16,2,2,4,256]{4,3,2,1,0:T(4,128)S(1)} async-done(((f32[16,2,2,4,256]{4,3,2,1,0:T(4,128)}), f32[16,2,2,4,256]{4,3,2,1,0:T(4,128)S(1)}, u32[]{:S(2)}, u32[]{:S(2)}) %all-to-all-start.2) | async-done | bytes 262176 | tf_op jit(solution)/shard_map/all_to_all | solution.py:193
  98.3 4.4 %all-to-all-start.1 = ((f32[16,2,2,4,256]{4,3,2,1,0:T(4,128)}), f32[16,2,2,4,256]{4,3,2,1,0:T(4,128)S(1)}, u32[]{:S(2)}, u32[]{:S(2)}) async-start(f32[16,2,2,4,256]{4,3,2,1,0:T(4,128)} %copy.80), calls=%async_computation.1 | async-start | bytes 524288 | tf_op jit(solution)/shard_map/all_to_all | solution.py:192
  102.8 6.4 %all-to-all-done.1 = f32[16,2,2,4,256]{4,3,2,1,0:T(4,128)S(1)} async-done(((f32[16,2,2,4,256]{4,3,2,1,0:T(4,128)}), f32[16,2,2,4,256]{4,3,2,1,0:T(4,128)S(1)}, u32[]{:S(2)}, u32[]{:S(2)}) %all-to-all-start.1) | async-done | bytes 262176 | tf_op jit(solution)/shard_map/all_to_all | solution.py:192
  109.3 7.4 %all_gather.16 = f32[2,4,2,32,256]{4,3,2,0,1:T(8,128)S(1)} all-gather(f32[2,2,2,32,256]{4,3,2,0,1:T(8,128)S(1)} %all_to_all.85), channel_id=1, replica_groups=mesh['step'=8,'node'=2,'space'=32] {'node'}, dimensions={1}, use_global_device_ids=true | all-gather | bytes 786432 | tf_op jit(solution)/shard_map/all_gather | solution.py:197
  116.7 6.6 %all_gather.17 = f32[2,4,2,32,256]{4,3,2,0,1:T(8,128)S(1)} all-gather(f32[2,2,2,32,256]{4,3,2,0,1:T(8,128)S(1)} %all_to_all.89), channel_id=1, replica_groups=mesh['step'=8,'node'=2,'space'=32] {'node'}, dimensions={1}, use_global_device_ids=true | all-gather | bytes 786432 | tf_op jit(solution)/shard_map/all_gather | solution.py:198
  141.5 4.7 %collective-permute-start.6 = (f32[2,2,2,1,32,256]{5,2,4,3,1,0:T(2,128)S(1)}, f32[2,2,2,1,32,256]{5,2,4,3,1,0:T(2,128)S(1)}, u32[]{:S(2)}, u32[]{:S(2)}) collective-permute-start(f32[2,2,2,1,32,256]{5,2,4,3,1,0:T(2,128)S(1)} %get-tuple-element.42), channel_id=1, source_target_pairs={{0,1},{1,2},{2,3},{3,4},{4,5},{5,6},{6,7},{7,8},{8,9},{9,10},{10,1... | collective-permute-start | bytes 786440 | tf_op jit(solution)/shard_map/ppermute | solution.py:24
  153.1 4.7 %collective-permute-start.8 = (f32[2,2,2,1,32,256]{5,2,4,3,1,0:T(2,128)S(1)}, f32[2,2,2,1,32,256]{5,2,4,3,1,0:T(2,128)S(1)}, u32[]{:S(2)}, u32[]{:S(2)}) collective-permute-start(f32[2,2,2,1,32,256]{5,2,4,3,1,0:T(2,128)S(1)} %get-tuple-element.40), channel_id=1, source_target_pairs={{0,1},{1,2},{2,3},{3,4},{4,5},{5,6},{6,7},{7,8},{8,9},{9,10},{10,1... | collective-permute-start | bytes 786440 | tf_op jit(solution)/shard_map/ppermute | solution.py:24
  164.8 4.5 %collective-permute-start.10 = (f32[2,2,2,1,32,256]{5,2,4,3,1,0:T(2,128)S(1)}, f32[2,2,2,1,32,256]{5,2,4,3,1,0:T(2,128)S(1)}, u32[]{:S(2)}, u32[]{:S(2)}) collective-permute-start(f32[2,2,2,1,32,256]{5,2,4,3,1,0:T(2,128)S(1)} %get-tuple-element.38), channel_id=1, source_target_pairs={{0,1},{1,2},{2,3},{3,4},{4,5},{5,6},{6,7},{7,8},{8,9},{9,10},{10,1... | collective-permute-start | bytes 786440 | tf_op jit(solution)/shard_map/ppermute | solution.py:24
  176.2 4.5 %collective-permute-start.12 = (f32[2,2,2,1,32,256]{5,2,4,3,1,0:T(2,128)S(1)}, f32[2,2,2,1,32,256]{5,2,4,3,1,0:T(2,128)S(1)}, u32[]{:S(2)}, u32[]{:S(2)}) collective-permute-start(f32[2,2,2,1,32,256]{5,2,4,3,1,0:T(2,128)S(1)} %get-tuple-element.36), channel_id=1, source_target_pairs={{0,1},{1,2},{2,3},{3,4},{4,5},{5,6},{6,7},{7,8},{8,9},{9,10},{10,1... | collective-permute-start | bytes 786440 | tf_op jit(solution)/shard_map/ppermute | solution.py:24
  187.6 5.6 %collective-permute-start.14 = (f32[2,2,2,1,32,256]{5,2,4,3,1,0:T(2,128)S(1)}, f32[2,2,2,1,32,256]{5,2,4,3,1,0:T(2,128)S(1)}, u32[]{:S(2)}, u32[]{:S(2)}) collective-permute-start(f32[2,2,2,1,32,256]{5,2,4,3,1,0:T(2,128)S(1)} %get-tuple-element.34), channel_id=1, source_target_pairs={{0,1},{1,2},{2,3},{3,4},{4,5},{5,6},{6,7},{7,8},{8,9},{9,10},{10,1... | collective-permute-start | bytes 786440 | tf_op jit(solution)/shard_map/ppermute | solution.py:24
  200.1 5.9 %collective-permute-start.16 = (f32[2,2,2,1,32,256]{5,2,4,3,1,0:T(2,128)S(1)}, f32[2,2,2,1,32,256]{5,2,4,3,1,0:T(2,128)S(1)}, u32[]{:S(2)}, u32[]{:S(2)}) collective-permute-start(f32[2,2,2,1,32,256]{5,2,4,3,1,0:T(2,128)S(1)} %get-tuple-element.32), channel_id=1, source_target_pairs={{0,1},{1,2},{2,3},{3,4},{4,5},{5,6},{6,7},{7,8},{8,9},{9,10},{10,1... | collective-permute-start | bytes 786440 | tf_op jit(solution)/shard_map/ppermute | solution.py:24
  212.3 57.9 %all-gather.2.cloned.1.call-done = f32[2,2,4,2,32,256]{5,4,3,1,0,2:T(8,128)} async-done(((f32[2,2,2,2,32,256]{5,4,3,1,0,2:T(8,128)}), f32[2,2,4,2,32,256]{5,4,3,1,0,2:T(8,128)}) %all-gather.2.cloned.1.call-update) | async-done | bytes 1048592 | tf_op jit(solution)/shard_map/all_gather | solution.py:210
  276.2 5.0 %all-to-all-start.4 = ((f32[2,2,2,32,256]{4,1,2,0,3:T(2,128)}), f32[2,2,2,32,256]{4,1,2,0,3:T(2,128)S(1)}, u32[]{:S(2)}, u32[]{:S(2)}) async-start(f32[2,2,2,32,256]{4,1,2,0,3:T(2,128)} %copy.93), calls=%async_computation.4 | async-start | bytes 524288 | tf_op jit(solution)/shard_map/all_to_all | solution.py:216
  283.2 4.4 %all-to-all-done.4 = f32[2,2,2,32,256]{4,1,2,0,3:T(2,128)S(1)} async-done(((f32[2,2,2,32,256]{4,1,2,0,3:T(2,128)}), f32[2,2,2,32,256]{4,1,2,0,3:T(2,128)S(1)}, u32[]{:S(2)}, u32[]{:S(2)}) %all-to-all-start.4) | async-done | bytes 262176 | tf_op jit(solution)/shard_map/all_to_all | solution.py:216
  287.7 4.4 %all-to-all-start.3 = ((f32[2,2,2,32,256]{4,1,2,0,3:T(2,128)}), f32[2,2,2,32,256]{4,1,2,0,3:T(2,128)S(1)}, u32[]{:S(2)}, u32[]{:S(2)}) async-start(f32[2,2,2,32,256]{4,1,2,0,3:T(2,128)} %copy.91), calls=%async_computation.3 | async-start | bytes 524288 | tf_op jit(solution)/shard_map/all_to_all | solution.py:215
  292.4 6.2 %all-to-all-done.3 = f32[2,2,2,32,256]{4,1,2,0,3:T(2,128)S(1)} async-done(((f32[2,2,2,32,256]{4,1,2,0,3:T(2,128)}), f32[2,2,2,32,256]{4,1,2,0,3:T(2,128)S(1)}, u32[]{:S(2)}, u32[]{:S(2)}) %all-to-all-start.3) | async-done | bytes 262176 | tf_op jit(solution)/shard_map/all_to_all | solution.py:215
  299.9 9.9 %all_to_all.109 = f32[16,2,2,4,256]{4,3,2,1,0:T(4,128)S(1)} all-to-all(f32[16,2,2,4,256]{4,3,2,1,0:T(4,128)S(1)} %copy.95), channel_id=1, replica_groups=mesh['step'=8,'node'=2,'space'=32] {'step'}, dimensions={0} | all-to-all | bytes 524288 | tf_op jit(solution)/shard_map/all_to_all | solution.py:223
  316.1 37.4 %all-reduce.23.cloned.1.call-done = f32[2,2,32,256]{3,2,1,0:T(8,128)} async-done(((f32[2,2,32,256]{3,2,1,0:T(8,128)}), f32[2,2,32,256]{3,2,1,0:T(8,128)}) %all-reduce.23.cloned.1.call-update) | async-done | bytes 131088 | tf_op jit(solution)/shard_map/psum | solution.py:32
  358.8 7.5 %all_gather.19 = f32[2,4,2,32,256]{4,3,2,0,1:T(8,128)S(1)} all-gather(f32[2,2,2,32,256]{4,3,2,0,1:T(8,128)S(1)} %copy.99), channel_id=1, replica_groups=mesh['step'=8,'node'=2,'space'=32] {'node'}, dimensions={1}, use_global_device_ids=true | all-gather | bytes 786432 | tf_op jit(solution)/shard_map/all_gather | solution.py:152
  (145 shorter events, 94.8 us)
Async XLA Ops:
  7.2 52.6 %all-reduce.21.cloned.1.call-start = ((), (), s32[]{:S(2)}) async-start(), calls=%async_computation.6 | async-start | bytes 262144 | tf_op jit(solution)/shard_map/psum | solution.py:32
  8.9 55.9 %collective-permute-start.1 = (f32[2,2,1,32,256]{4,3,2,1,0:T(8,128)S(1)}, f32[2,2,1,32,256]{4,3,2,1,0:T(8,128)S(1)}, u32[]{:S(2)}, u32[]{:S(2)}) collective-permute-start(f32[2,2,1,32,256]{4,3,2,1,0:T(8,128)S(1)} %get-tuple-element.47), channel_id=1, source_target_pairs={{1,0},{2,1},{3,2},{4,3},{5,4},{6,5},{7,6},{8,7},{9,8},{10,9},{11,1... | collective-permute-start | bytes 393224 | tf_op jit(solution)/shard_map/ppermute | solution.py:25
  10.2 54.6 %collective-permute-start.2 = (f32[2,2,1,32,256]{4,3,2,1,0:T(8,128)S(1)}, f32[2,2,1,32,256]{4,3,2,1,0:T(8,128)S(1)}, u32[]{:S(2)}, u32[]{:S(2)}) collective-permute-start(f32[2,2,1,32,256]{4,3,2,1,0:T(8,128)S(1)} %get-tuple-element.48), channel_id=1, source_target_pairs={{0,1},{1,2},{2,3},{3,4},{4,5},{5,6},{6,7},{7,8},{8,9},{9,10},{10,1... | collective-permute-start | bytes 393224 | tf_op jit(solution)/shard_map/ppermute | solution.py:24
  60.6 13.2 %collective-permute-start = (f32[1,2,32,256]{3,2,1,0:T(8,128)S(1)}, f32[1,2,32,256]{3,2,1,0:T(8,128)S(1)}, u32[]{:S(2)}, u32[]{:S(2)}) collective-permute-start(f32[1,2,32,256]{3,2,1,0:T(8,128)S(1)} %get-tuple-element.51), channel_id=1, source_target_pairs={{0,64},{64,128},{128,192},{192,256},{256,320},{320,384},{384,448},... | collective-permute-start | bytes 196616 | tf_op jit(solution)/shard_map/ppermute | solution.py:38
  87.4 10.9 %all-to-all-start.2 = ((f32[16,2,2,4,256]{4,3,2,1,0:T(4,128)}), f32[16,2,2,4,256]{4,3,2,1,0:T(4,128)S(1)}, u32[]{:S(2)}, u32[]{:S(2)}) async-start(f32[16,2,2,4,256]{4,3,2,1,0:T(4,128)} %copy.83), calls=%async_computation.2 | async-start | bytes 524288 | tf_op jit(solution)/shard_map/all_to_all | solution.py:193
  98.3 10.9 %all-to-all-start.1 = ((f32[16,2,2,4,256]{4,3,2,1,0:T(4,128)}), f32[16,2,2,4,256]{4,3,2,1,0:T(4,128)S(1)}, u32[]{:S(2)}, u32[]{:S(2)}) async-start(f32[16,2,2,4,256]{4,3,2,1,0:T(4,128)} %copy.80), calls=%async_computation.1 | async-start | bytes 524288 | tf_op jit(solution)/shard_map/all_to_all | solution.py:192
  102.6 167.5 %all-gather.2.cloned.1.call-start = ((), (), s32[]{:S(2)}) async-start(), calls=%async_computation.7 | async-start | bytes 1572864 | tf_op jit(solution)/shard_map/all_gather | solution.py:210
  140.2 7.9 %collective-permute-start.5 = (f32[2,2,2,1,32,256]{5,2,4,3,1,0:T(2,128)S(1)}, f32[2,2,2,1,32,256]{5,2,4,3,1,0:T(2,128)S(1)}, u32[]{:S(2)}, u32[]{:S(2)}) collective-permute-start(f32[2,2,2,1,32,256]{5,2,4,3,1,0:T(2,128)S(1)} %get-tuple-element.41), channel_id=1, source_target_pairs={{1,0},{2,1},{3,2},{4,3},{5,4},{6,5},{7,6},{8,7},{9,8},{10,9},{11,1... | collective-permute-start | bytes 786440 | tf_op jit(solution)/shard_map/ppermute | solution.py:25
  141.5 8.0 %collective-permute-start.6 = (f32[2,2,2,1,32,256]{5,2,4,3,1,0:T(2,128)S(1)}, f32[2,2,2,1,32,256]{5,2,4,3,1,0:T(2,128)S(1)}, u32[]{:S(2)}, u32[]{:S(2)}) collective-permute-start(f32[2,2,2,1,32,256]{5,2,4,3,1,0:T(2,128)S(1)} %get-tuple-element.42), channel_id=1, source_target_pairs={{0,1},{1,2},{2,3},{3,4},{4,5},{5,6},{6,7},{7,8},{8,9},{9,10},{10,1... | collective-permute-start | bytes 786440 | tf_op jit(solution)/shard_map/ppermute | solution.py:24
  151.8 7.9 %collective-permute-start.7 = (f32[2,2,2,1,32,256]{5,2,4,3,1,0:T(2,128)S(1)}, f32[2,2,2,1,32,256]{5,2,4,3,1,0:T(2,128)S(1)}, u32[]{:S(2)}, u32[]{:S(2)}) collective-permute-start(f32[2,2,2,1,32,256]{5,2,4,3,1,0:T(2,128)S(1)} %get-tuple-element.39), channel_id=1, source_target_pairs={{1,0},{2,1},{3,2},{4,3},{5,4},{6,5},{7,6},{8,7},{9,8},{10,9},{11,1... | collective-permute-start | bytes 786440 | tf_op jit(solution)/shard_map/ppermute | solution.py:25
  153.1 8.0 %collective-permute-start.8 = (f32[2,2,2,1,32,256]{5,2,4,3,1,0:T(2,128)S(1)}, f32[2,2,2,1,32,256]{5,2,4,3,1,0:T(2,128)S(1)}, u32[]{:S(2)}, u32[]{:S(2)}) collective-permute-start(f32[2,2,2,1,32,256]{5,2,4,3,1,0:T(2,128)S(1)} %get-tuple-element.40), channel_id=1, source_target_pairs={{0,1},{1,2},{2,3},{3,4},{4,5},{5,6},{6,7},{7,8},{8,9},{9,10},{10,1... | collective-permute-start | bytes 786440 | tf_op jit(solution)/shard_map/ppermute | solution.py:24
  163.5 7.6 %collective-permute-start.9 = (f32[2,2,2,1,32,256]{5,2,4,3,1,0:T(2,128)S(1)}, f32[2,2,2,1,32,256]{5,2,4,3,1,0:T(2,128)S(1)}, u32[]{:S(2)}, u32[]{:S(2)}) collective-permute-start(f32[2,2,2,1,32,256]{5,2,4,3,1,0:T(2,128)S(1)} %get-tuple-element.37), channel_id=1, source_target_pairs={{1,0},{2,1},{3,2},{4,3},{5,4},{6,5},{7,6},{8,7},{9,8},{10,9},{11,1... | collective-permute-start | bytes 786440 | tf_op jit(solution)/shard_map/ppermute | solution.py:25
  164.8 7.7 %collective-permute-start.10 = (f32[2,2,2,1,32,256]{5,2,4,3,1,0:T(2,128)S(1)}, f32[2,2,2,1,32,256]{5,2,4,3,1,0:T(2,128)S(1)}, u32[]{:S(2)}, u32[]{:S(2)}) collective-permute-start(f32[2,2,2,1,32,256]{5,2,4,3,1,0:T(2,128)S(1)} %get-tuple-element.38), channel_id=1, source_target_pairs={{0,1},{1,2},{2,3},{3,4},{4,5},{5,6},{6,7},{7,8},{8,9},{9,10},{10,1... | collective-permute-start | bytes 786440 | tf_op jit(solution)/shard_map/ppermute | solution.py:24
  176.2 7.7 %collective-permute-start.12 = (f32[2,2,2,1,32,256]{5,2,4,3,1,0:T(2,128)S(1)}, f32[2,2,2,1,32,256]{5,2,4,3,1,0:T(2,128)S(1)}, u32[]{:S(2)}, u32[]{:S(2)}) collective-permute-start(f32[2,2,2,1,32,256]{5,2,4,3,1,0:T(2,128)S(1)} %get-tuple-element.36), channel_id=1, source_target_pairs={{0,1},{1,2},{2,3},{3,4},{4,5},{5,6},{6,7},{7,8},{8,9},{9,10},{10,1... | collective-permute-start | bytes 786440 | tf_op jit(solution)/shard_map/ppermute | solution.py:24
  186.3 8.7 %collective-permute-start.13 = (f32[2,2,2,1,32,256]{5,2,4,3,1,0:T(2,128)S(1)}, f32[2,2,2,1,32,256]{5,2,4,3,1,0:T(2,128)S(1)}, u32[]{:S(2)}, u32[]{:S(2)}) collective-permute-start(f32[2,2,2,1,32,256]{5,2,4,3,1,0:T(2,128)S(1)} %get-tuple-element.33), channel_id=1, source_target_pairs={{1,0},{2,1},{3,2},{4,3},{5,4},{6,5},{7,6},{8,7},{9,8},{10,9},{11,1... | collective-permute-start | bytes 786440 | tf_op jit(solution)/shard_map/ppermute | solution.py:25
  187.6 8.9 %collective-permute-start.14 = (f32[2,2,2,1,32,256]{5,2,4,3,1,0:T(2,128)S(1)}, f32[2,2,2,1,32,256]{5,2,4,3,1,0:T(2,128)S(1)}, u32[]{:S(2)}, u32[]{:S(2)}) collective-permute-start(f32[2,2,2,1,32,256]{5,2,4,3,1,0:T(2,128)S(1)} %get-tuple-element.34), channel_id=1, source_target_pairs={{0,1},{1,2},{2,3},{3,4},{4,5},{5,6},{6,7},{7,8},{8,9},{9,10},{10,1... | collective-permute-start | bytes 786440 | tf_op jit(solution)/shard_map/ppermute | solution.py:24
  198.8 8.8 %collective-permute-start.15 = (f32[2,2,2,1,32,256]{5,2,4,3,1,0:T(2,128)S(1)}, f32[2,2,2,1,32,256]{5,2,4,3,1,0:T(2,128)S(1)}, u32[]{:S(2)}, u32[]{:S(2)}) collective-permute-start(f32[2,2,2,1,32,256]{5,2,4,3,1,0:T(2,128)S(1)} %get-tuple-element.31), channel_id=1, source_target_pairs={{1,0},{2,1},{3,2},{4,3},{5,4},{6,5},{7,6},{8,7},{9,8},{10,9},{11,1... | collective-permute-start | bytes 786440 | tf_op jit(solution)/shard_map/ppermute | solution.py:25
  200.1 9.0 %collective-permute-start.16 = (f32[2,2,2,1,32,256]{5,2,4,3,1,0:T(2,128)S(1)}, f32[2,2,2,1,32,256]{5,2,4,3,1,0:T(2,128)S(1)}, u32[]{:S(2)}, u32[]{:S(2)}) collective-permute-start(f32[2,2,2,1,32,256]{5,2,4,3,1,0:T(2,128)S(1)} %get-tuple-element.32), channel_id=1, source_target_pairs={{0,1},{1,2},{2,3},{3,4},{4,5},{5,6},{6,7},{7,8},{8,9},{9,10},{10,1... | collective-permute-start | bytes 786440 | tf_op jit(solution)/shard_map/ppermute | solution.py:24
  276.2 11.5 %all-to-all-start.4 = ((f32[2,2,2,32,256]{4,1,2,0,3:T(2,128)}), f32[2,2,2,32,256]{4,1,2,0,3:T(2,128)S(1)}, u32[]{:S(2)}, u32[]{:S(2)}) async-start(f32[2,2,2,32,256]{4,1,2,0,3:T(2,128)} %copy.93), calls=%async_computation.4 | async-start | bytes 524288 | tf_op jit(solution)/shard_map/all_to_all | solution.py:216
  287.7 10.9 %all-to-all-start.3 = ((f32[2,2,2,32,256]{4,1,2,0,3:T(2,128)}), f32[2,2,2,32,256]{4,1,2,0,3:T(2,128)S(1)}, u32[]{:S(2)}, u32[]{:S(2)}) async-start(f32[2,2,2,32,256]{4,1,2,0,3:T(2,128)} %copy.91), calls=%async_computation.3 | async-start | bytes 524288 | tf_op jit(solution)/shard_map/all_to_all | solution.py:215
  292.0 61.4 %all-reduce.23.cloned.1.call-start = ((), (), s32[]{:S(2)}) async-start(), calls=%async_computation.8 | async-start | bytes 262144 | tf_op jit(solution)/shard_map/psum | solution.py:32
  310.8 47.7 %collective-permute-start.18 = (f32[2,2,1,32,256]{4,3,2,1,0:T(8,128)S(1)}, f32[2,2,1,32,256]{4,3,2,1,0:T(8,128)S(1)}, u32[]{:S(2)}, u32[]{:S(2)}) collective-permute-start(f32[2,2,1,32,256]{4,3,2,1,0:T(8,128)S(1)} %get-tuple-element.45), channel_id=1, source_target_pairs={{1,0},{2,1},{3,2},{4,3},{5,4},{6,5},{7,6},{8,7},{9,8},{10,9},{11,1... | collective-permute-start | bytes 393224 | tf_op jit(solution)/shard_map/ppermute | solution.py:25
  312.1 46.4 %collective-permute-start.19 = (f32[2,2,1,32,256]{4,3,2,1,0:T(8,128)S(1)}, f32[2,2,1,32,256]{4,3,2,1,0:T(8,128)S(1)}, u32[]{:S(2)}, u32[]{:S(2)}) collective-permute-start(f32[2,2,1,32,256]{4,3,2,1,0:T(8,128)S(1)} %get-tuple-element.46), channel_id=1, source_target_pairs={{0,1},{1,2},{2,3},{3,4},{4,5},{5,6},{6,7},{7,8},{8,9},{9,10},{10,1... | collective-permute-start | bytes 393224 | tf_op jit(solution)/shard_map/ppermute | solution.py:24
  354.3 13.2 %collective-permute-start.17 = (f32[1,2,32,256]{3,2,1,0:T(8,128)S(1)}, f32[1,2,32,256]{3,2,1,0:T(8,128)S(1)}, u32[]{:S(2)}, u32[]{:S(2)}) collective-permute-start(f32[1,2,32,256]{3,2,1,0:T(8,128)S(1)} %get-tuple-element.49), channel_id=1, source_target_pairs={{0,64},{64,128},{128,192},{192,256},{256,320},{320,384},{384,448},... | collective-permute-start | bytes 196616 | tf_op jit(solution)/shard_map/ppermute | solution.py:38
  (10 other events, 165.5 us)
Sparse Core Ops, SparseCore 0:
  11.4 48.2 all-reduce.20
  212.4 57.7 all-gather.1
  310.9 42.5 all-reduce.22
where the time goes:
time: 376 us; the launch traced here: 375 us
  waiting for transfers between devices  182 us (48%)
  starting transfers between devices  81 us (22%)
  blocking collectives  50.5 us (13%)
  other arithmetic  22.3 us (6%)
  between operations  15.2 us (4%)
  matrix products  14.8 us (4%)
  local copies, waits for them, and re-layouts  8.91 us (2%)
    psum x2, waiting for transfers between devices, spread(): return lax.psum(kept, axis)  81.2 us
    all_gather x1, waiting for transfers between devices, on_device(): shard_piece = lax.all_gather(solved, 'node', axis=2, tiled=True)  57.9 us
    ppermute x9, starting transfers between devices, padded_2(): before = lax.ppermute(last, axis, up)  43.1 us
    all_gather x2, blocking collectives, reaction_residual(): shard_piece = lax.all_gather(forcing, 'node', axis=1, tiled=True)  14.9 us
    ppermute x9, starting transfers between devices, padded_2(): after = lax.ppermute(leading, axis, down)  11.6 us
    all_to_all x1, blocking collectives, on_device(): lax.all_to_all(scaled, 'step', split_axis=3, concat_axis=0, tiled=True)  11.6 us
    ppermute x9, waiting for transfers between devices, padded_2(): before = lax.ppermute(last, axis, up)  10.3 us
    ppermute x9, waiting for transfers between devices, padded_2(): after = lax.ppermute(leading, axis, down)  10.3 us
  transfers between devices with their start and end apart: 27, of which 21 were waited for; matrix products, arithmetic and copies ran while one was open for 3% of the time, Pallas kernels for 0%

commit v1 on v0

v1 whole, which is shorter than its diff:
```python
import math

import jax
import jax.numpy as jnp
import numpy as np
from jax import lax
from jax.sharding import PartitionSpec as P

STEPS = 16
NODES = 4
SWEEPS = 8
GX = 32
GY = 256
NZ = 64

DIFFUSION = 0.5
REACTION = 1.0
HIGH = lax.Precision.HIGHEST


def legendre_pair(degree, point):
    previous_term, current_term = (1.0, point)
    for degree_now in range(1, degree):
        previous_term, current_term = (
            current_term,
            ((2 * degree_now + 1) * point * current_term - degree_now * previous_term)
            / (degree_now + 1),
        )
    return (current_term, previous_term)


def radau_value(count, point):
    high_term, low_term = legendre_pair(count, point)
    return high_term - low_term


def radau_points(count):
    roots_found = []
    samples = 4000
    for sample_index in range(samples):
        left_end = -1.0 + 2.0 * sample_index / samples
        right_end = -1.0 + 2.0 * (sample_index + 1) / samples
        if radau_value(count, left_end) * radau_value(count, right_end) < 0.0:
            for halving in range(200):
                middle = 0.5 * (left_end + right_end)
                if radau_value(count, left_end) * radau_value(count, middle) <= 0.0:
                    right_end = middle
                else:
                    left_end = middle
            roots_found.append(0.5 * (left_end + right_end))
    roots_found.append(1.0)
    return [(root_value + 1.0) / 2.0 for root_value in roots_found]


def collocation_matrix(node_count):
    points = radau_points(node_count)
    node_table = [[0.0] * node_count for row_number in range(node_count)]
    for column in range(node_count):
        coeffs = [1.0]
        for another in range(node_count):
            if another != column:
                spacing = points[column] - points[another]
                raised = [0.0] + coeffs
                lowered = [entry * points[another] for entry in coeffs] + [0.0]
                coeffs = [
                    (first_entry - second_entry) / spacing
                    for first_entry, second_entry in zip(raised, lowered)
                ]
        integral = [0.0] + [
            entry / (exponent_index + 1) for exponent_index, entry in enumerate(coeffs)
        ]
        for row_number in range(node_count):
            running = 0.0
            for exponent_index in range(len(integral) - 1, -1, -1):
                running = running * points[row_number] + integral[exponent_index]
            node_table[row_number][column] = running
    return node_table


def sine_matrix(count):
    index = np.arange(1, count + 1)
    return math.sqrt(2.0 / (count + 1)) * np.sin(np.pi * np.outer(index, index) / (count + 1))


def eigenvalues(count):
    return 2.0 * np.cos(np.pi * np.arange(1, count + 1) / (count + 1))


def tables():
    coll = np.array(collocation_matrix(NODES))
    sx, sy, sz = (sine_matrix(n) for n in (GX, GY, NZ))
    kx = np.einsum("kx,fg->kfgx", sx, np.eye(8)).reshape(256, 256)
    n = np.arange(STEPS)
    real_dft = np.zeros((8, 2, STEPS))
    for q in range(8):
        real_dft[q, 0] = np.cos(2 * np.pi * q * n / STEPS)
        real_dft[q, 1] = -np.sin(2 * np.pi * q * n / STEPS) if q else np.cos(np.pi * n)
    shifted = np.zeros_like(real_dft)
    shifted[:, :, :-1] = real_dft[:, :, 1:]
    split = real_dft.reshape(8, 2, 8, 2)
    shifted = shifted.reshape(8, 2, 8, 2)
    nodes = np.eye(NODES).reshape(NODES, 2, 2)
    last = np.zeros((NODES, 2, 2))
    last[:, 1, 1] = 1.0
    two = np.eye(2)
    form = "qrsn,mtj,kl,zw->qkrmzstlnjw"
    mu0 = -np.einsum(form, split, nodes, two, two).reshape(256, 256)
    mu1 = np.einsum(form, shifted, last, two, two).reshape(256, 256)
    mf = np.einsum(form, split, coll.reshape(NODES, 2, 2), two, two).reshape(256, 256)
    mi = np.einsum("qrsn,mtj,kl,zw->stlnjwqkrmz", split, nodes, two, two).reshape(256, 256)
    zf = np.einsum("rp,mn,ksz->rmkspnz", two, np.eye(4), sz.reshape(NZ, 32, 2)).reshape(512, 512)
    lam_z, lam_x, lam_y = (eigenvalues(n) for n in (NZ, GX, GY))
    start = np.linalg.solve(coll, np.ones(NODES))
    return dict(coll=coll, sy=sy, kx=kx, mu0=mu0, mu1=mu1, mf=mf, mi=mi, zf=zf, lam_z=lam_z,
                lam_x=lam_x, lam_y=lam_y, start=start)


TABLES = tables()


def table(name):
    return jnp.asarray(TABLES[name], jnp.float32)


def dot(a, b):
    return jnp.dot(a, b, precision=HIGH, preferred_element_type=jnp.float32)


def in_plane(v):
    out = jnp.zeros_like(v)
    pad = [(0, 0)] * (v.ndim - 2)
    a = jnp.pad(v, pad + [(1, 1), (0, 0)])
    b = jnp.pad(v, pad + [(0, 0), (1, 1)])
    return a[..., 2:, :] + a[..., :-2, :] + b[..., 2:] + b[..., :-2]


def on_device(iterate, initial_value, alpha_power, node_mix, node_back, shifts):
    step, node, space = (lax.axis_index(a) for a in ("step", "node", "space"))
    ring_up = [(i, (i + 1)) for i in range(31)]
    ring_down = [(i + 1, i) for i in range(31)]
    below = lax.ppermute(iterate[:, :, 1:], "space", ring_up)
    above = lax.ppermute(iterate[:, :, :1], "space", ring_down)
    padded = jnp.concatenate([below, iterate, above], 2)
    nb = padded[:, :, 2:] + padded[:, :, :-2] + in_plane(iterate)
    forcing = DIFFUSION * (nb - 6.0 * iterate) + REACTION * (iterate - iterate * iterate * iterate)
    start = lax.dynamic_slice_in_dim(table("start"), node * 2, 2)
    first = jnp.where(step == 0, start, 0.0)[:, None, None, None] * initial_value[None]
    forcing = jnp.concatenate([forcing[:1] + first[None], forcing[1:]], 0)

    sy, kx = table("sy"), table("kx")
    uh = dot(kx, dot(iterate.reshape(256, 256), sy))
    fh = dot(kx, dot(forcing.reshape(256, 256), sy))
    sent = jnp.stack([uh.reshape(16, 16, 256), fh.reshape(16, 16, 256)], 1)
    got = lax.all_to_all(sent, ("step", "node"), 0, 0, tiled=True)
    ru, rf = got[:, 0].reshape(256, 256), got[:, 1].reshape(256, 256)

    exponent = alpha_power[0].astype(jnp.float32) / 16.0 / STEPS
    n_of = (np.arange(256) // 32) * 2 + (np.arange(256) // 4) % 2
    n_of = jnp.asarray(n_of, jnp.float32)
    scale0 = jnp.exp2(-exponent * n_of)
    scale1 = jnp.exp2(-exponent * (n_of + 1.0))
    mu = table("mu0") * scale0[None] + table("mu1") * scale1[None]
    mf = table("mf") * scale0[None]
    spec = dot(mu, ru) + dot(mf, rf)

    spec = spec.reshape(16, 16, 2, 128).transpose(0, 2, 1, 3).reshape(32, 16, 128)
    spec = lax.all_to_all(spec, "space", 0, 0, tiled=True).reshape(512, 128)
    s = dot(table("zf"), spec).reshape(2, 4, 64, 128)

    q = space // 4
    kk = (space // 2) % 2
    h = space % 2
    p = step * 2 + node
    params = [lax.all_gather(lax.all_gather(x, "step", axis=1, tiled=True), "node", axis=2, tiled=True)
              for x in (node_mix, node_back, shifts)]
    def of(x, k):
        return lax.complex(*[lax.dynamic_index_in_dim(x[c], k, 0, keepdims=False) for c in (0, 1)])
    def coefs(k):
        d = of(params[2], k)
        b = 1.0 + 2.0 * d
        r = 0.5 * d / b
        g = jnp.stack([r ** j / b for j in range(SWEEPS)])
        return jnp.sum(of(params[1], k)[None, :, :, None] * g[:, None, :, None] * of(params[0], k)[None, None], 2)
    ck, cp = coefs(q), coefs(jnp.where(q == 0, 8, 16 - q))
    ca = jnp.where(q == 0, ck.real, ck.real + cp.real)
    ce = jnp.where(q == 0, 0.0, ck.imag - cp.imag)
    cd = jnp.where(q == 0, cp.real, ck.real + cp.real)
    lam_x = lax.dynamic_index_in_dim(table("lam_x"), 2 * p + kk, 0, keepdims=False)
    lam_y = lax.dynamic_slice_in_dim(table("lam_y"), h * 128, 128)
    lam = table("lam_z")[:, None] + lam_y[None] + lam_x
    def horner(c):
        acc = c[-1]
        for j in range(SWEEPS - 2, -1, -1):
            acc = acc * lam + c[j]
        return acc
    def apply(c, v):
        return jnp.stack([sum(horner(c[:, i, j]) * v[j] for j in range(4)) for i in range(4)])
    out = jnp.stack([apply(ca, s[0]) - apply(ce, s[1]), apply(ce, s[0]) + apply(cd, s[1])])

    back = dot(table("zf").T, out.reshape(512, 128)).reshape(32, 16, 128)
    back = lax.all_to_all(back, "space", 0, 0, tiled=True)
    back = back.reshape(16, 2, 16, 128).transpose(0, 2, 1, 3).reshape(256, 256)
    mi = table("mi") * (jnp.exp2(exponent * n_back()) / STEPS)[:, None]
    corr = dot(mi, back).reshape(8, 1, 2, 16, 256)
    corr = jnp.broadcast_to(corr, (8, 2, 2, 16, 256)).reshape(16, 2, 16, 256)
    corr = lax.all_to_all(corr, ("step", "node"), 0, 0, tiled=True)
    corr = corr.transpose(1, 0, 2, 3).reshape(2, 256, 256)
    corr = jnp.stack([dot(dot(kx.T, corr[g]), sy) for g in range(2)]).reshape(2, 2, 2, 2, 32, 256)

    other = lax.ppermute(iterate, "node", [(0, 1), (1, 0)])
    both = jnp.where(node == 0, jnp.stack([iterate, other]), jnp.stack([other, iterate]))
    both = both + corr
    updated = lax.dynamic_index_in_dim(both, node, 0, keepdims=False)
    u = both.transpose(1, 0, 2, 3, 4, 5).reshape(2, 4, 2, 32, 256)
    rows = lax.dynamic_slice_in_dim(table("coll"), node * 2, 2, 0)
    mixed = DIFFUSION * (in_plane(u) + u[:, :, ::-1]) + (REACTION - 6.0 * DIFFUSION) * u - REACTION * u * u * u
    mixed = jnp.einsum("mj,njzxy->nmzxy", rows, mixed, precision=HIGH)
    edge = DIFFUSION * jnp.einsum("mj,njzxy->nmzxy", rows, u, precision=HIGH)
    below = lax.ppermute(edge[:, :, 1:], "space", ring_up)
    above = lax.ppermute(edge[:, :, :1], "space", ring_down)
    mixed = mixed + jnp.concatenate([below, above], 2)
    before = lax.ppermute(u[1, 3], "step", [(i, i + 1) for i in range(7)])
    before = jnp.where(step == 0, initial_value, before)
    previous = jnp.stack([before, u[0, 3]])
    return updated, previous[:, None] + mixed - updated


def n_back():
    return jnp.asarray((np.arange(256) // 32) * 2 + (np.arange(256) // 4) % 2, jnp.float32)


def solution(mesh):
    in_specs = (
        P("step", "node", "space", None, None),
        P("space", None, None),
        P(),
        P(None, "step", "node", None),
        P(None, "step", "node", None),
        P(None, "step", "node"),
    )
    out_specs = (P("step", "node", "space", None, None), P("step", "node", "space", None, None))
    return jax.shard_map(
        on_device, mesh=mesh, in_specs=in_specs, out_specs=out_specs, check_vma=False
    )
```

time: 376 us -> 537 us (1.43)
  other arithmetic: 22.3 us -> 335 us
  waiting for transfers between devices: 182 us -> 52.8 us
  starting transfers between devices: 81 us -> 48.8 us
  local copies, waits for them, and re-layouts: 8.91 us -> 26.9 us
  between operations: 15.2 us -> 2 us
    another operation x30 -> x20, other arithmetic: 9.07 us -> 333 us  [the longest x16 332 us: apply(): jnp.stack([sum((horner(c[:, i, j]) * v[j] for j in range(4))) for i in ra...]
    psum x2 -> x0, waiting for transfers between devices: 81.2 us -> none  [spread(): return lax.psum(kept, axis)]
    all_gather x1 -> x0, waiting for transfers between devices: 57.9 us -> none  [on_device(): shard_piece = lax.all_gather(solved, 'node', axis=2, tiled=True)]
    ppermute x20 -> x6, starting transfers between devices: 62.9 us -> 17.2 us  [the longest x1 5.01 us: on_device(): below = lax.ppermute(iterate[:, :, 1:], 'space', ring_up)]
    all_gather x4 -> x6, blocking collectives: 29 us -> 54.9 us  [the longest x3 45.4 us: on_device(): lax.all_gather(x, 'step', axis=1, tiled=True)]
    all_to_all x4, waiting for transfers between devices: 22.2 us -> 47.4 us  [the longest x1 19.7 us: on_device(): back = lax.all_to_all(back, 'space', 0, 0, tiled=True)]
    all_to_all x2 -> x0, blocking collectives: 21.5 us -> none  [the longest x1 11.6 us: on_device(): lax.all_to_all(scaled, 'step', split_axis=3, concat_axis=0, tiled=True)]
    ppermute x20 -> x6, waiting for transfers between devices: 20.7 us -> 5.46 us  [the longest x1 4.03 us: on_device(): above = lax.ppermute(edge[:, :, :1], 'space', ring_down)]
  transfers between devices with their start and end apart: 27 -> 10, of which waited for: 21 -> 6; matrix products, arithmetic and copies ran while one was open for 3% -> 4% of each run, Pallas kernels for 0% -> 0%
where the time goes in v1:
time: 537 us; the launch traced here: 532 us
  other arithmetic  335 us (62%)
  blocking collectives  54.9 us (10%)
  waiting for transfers between devices  52.8 us (10%)
  starting transfers between devices  48.8 us (9%)
  local copies, waits for them, and re-layouts  26.9 us (5%)
  matrix products  11.7 us (2%)
    another operation x16, other arithmetic, apply(): jnp.stack([sum((horner(c[:, i, j]) * v[j] for j in range(4))) for i in ra...  332 us
    all_gather x3, blocking collectives, on_device(): lax.all_gather(x, 'step', axis=1, tiled=True)  45.4 us
    all_to_all x1, waiting for transfers between devices, on_device(): back = lax.all_to_all(back, 'space', 0, 0, tiled=True)  19.7 us
    all_to_all x1, waiting for transfers between devices, on_device(): spec = lax.all_to_all(spec, 'space', 0, 0, tiled=True).reshape(512, 128)  15.3 us
    all_to_all x1, starting transfers between devices, on_device(): spec = lax.all_to_all(spec, 'space', 0, 0, tiled=True).reshape(512, 128)  13.7 us
    slice x18, local copies, waits for them, and re-layouts, horner(): acc = acc * lam + c[j]  12.9 us
  transfers between devices with their start and end apart: 10, of which 6 were waited for; matrix products, arithmetic and copies ran while one was open for 4% of the time, Pallas kernels for 0%

profile of v1, /device:TPU:1, one launch (start us, length us, event | category | flops | bytes accessed | tf_op | source)
XLA Modules:
  0.0 531.7 jit_solution(8190966689818724274)
XLA Ops:
  9.4 17.4 %all_gather.20 = f32[2,16,2]{2,0,1:T(2,128)S(1)} all-gather(f32[2,2,2]{2,0,1:T(2,128)S(1)} %copy.84), channel_id=1, replica_groups=mesh['step'=8,'node'=2,'space'=32] {'step'}, dimensions={1}, use_global_device_ids=true | all-gather | bytes 288 | tf_op jit(solution)/shard_map/all_gather | solution.py:174
  31.0 14.0 %all_gather.18 = f32[2,16,2,4]{3,2,0,1:T(2,128)S(1)} all-gather(f32[2,2,2,4]{3,2,0,1:T(2,128)S(1)} %copy.82), channel_id=1, replica_groups=mesh['step'=8,'node'=2,'space'=32] {'step'}, dimensions={1}, use_global_device_ids=true | all-gather | bytes 1152 | tf_op jit(solution)/shard_map/all_gather | solution.py:174
  48.2 14.0 %all_gather.22 = f32[2,16,2,4]{3,2,0,1:T(2,128)S(1)} all-gather(f32[2,2,2,4]{3,2,0,1:T(2,128)S(1)} %copy.88), channel_id=1, replica_groups=mesh['step'=8,'node'=2,'space'=32] {'step'}, dimensions={1}, use_global_device_ids=true | all-gather | bytes 1152 | tf_op jit(solution)/shard_map/all_gather | solution.py:174
  86.8 6.2 %all-to-all-done = f32[16,2,16,256]{3,2,1,0:T(8,128)S(1)} async-done(((f32[16,2,16,256]{3,2,1,0:T(8,128)}), f32[16,2,16,256]{3,2,1,0:T(8,128)S(1)}, u32[]{:S(2)}, u32[]{:S(2)}) %all-to-all-start) | async-done | bytes 524320 | tf_op jit(solution)/shard_map/all_to_all | solution.py:154
  95.3 13.7 %all-to-all-start.1 = ((f32[32,16,128]{2,1,0:T(8,128)}), f32[32,16,128]{2,1,0:T(8,128)S(1)}, u32[]{:S(2)}, u32[]{:S(2)}) async-start(f32[32,16,128]{2,1,0:T(8,128)} %bitcast.22), calls=%async_computation.1 | async-start | bytes 524288 | tf_op jit(solution)/shard_map/all_to_all | solution.py:167
  115.4 15.3 %all-to-all-done.1 = f32[32,16,128]{2,1,0:T(8,128)S(1)} async-done(((f32[32,16,128]{2,1,0:T(8,128)}), f32[32,16,128]{2,1,0:T(8,128)S(1)}, u32[]{:S(2)}, u32[]{:S(2)}) %all-to-all-start.1) | async-done | bytes 262176 | tf_op jit(solution)/shard_map/all_to_all | solution.py:167
  132.4 20.6 %add_bitcast_fusion.7 = f32[1,1,64,128]{3,2,1,0:T(8,128)S(1)} fusion(f32[512,128]{1,0:T(8,128)S(1)} %fusion.134, f32[]{:T(128)} %bitcast.179, f32[]{:T(128)} %bitcast.178, f32[]{:T(128)} %bitcast.177, f32[]{:T(128)} %bitcast.176, f32[]{:T(128)} %bitcast.175, f32[]{:T(128)} %bitcast.174, f32[]{:T(128)} %bitcast.173, f32[]{:T(128)} %bitcast.172, f32[]{:T(128)} %bitcast.171, ...), kind=kLoop, calls=%fused_computation.68 | loop fusion | flops 532480 | bytes 164740 | tf_op jit(solution)/shard_map/stack | solution.py:197
  153.0 20.6 %add_bitcast_fusion.11 = f32[1,1,64,128]{3,2,1,0:T(8,128)S(1)} fusion(f32[512,128]{1,0:T(8,128)S(1)} %fusion.134, f32[]{:T(128)} %bitcast.179, f32[]{:T(128)} %bitcast.178, f32[]{:T(128)} %bitcast.177, f32[]{:T(128)} %bitcast.176, f32[]{:T(128)} %bitcast.175, f32[]{:T(128)} %bitcast.174, f32[]{:T(128)} %bitcast.173, f32[]{:T(128)} %bitcast.172, ...), kind=kLoop, calls=%fused_computation.84 | loop fusion | flops 532480 | bytes 164740 | tf_op jit(solution)/shard_map/stack | solution.py:197
  173.7 21.0 %add_bitcast_fusion.6 = f32[1,1,64,128]{3,2,1,0:T(8,128)S(1)} fusion(f32[512,128]{1,0:T(8,128)S(1)} %fusion.134, f32[]{:T(128)} %bitcast.212, f32[]{:T(128)} %bitcast.211, f32[]{:T(128)} %bitcast.210, f32[]{:T(128)} %bitcast.209, f32[]{:T(128)} %bitcast.208, f32[]{:T(128)} %bitcast.207, f32[]{:T(128)} %bitcast.206, f32[]{:T(128)} %bitcast.205, f32[]{:T(128)} %bitcast.204, ...), kind=kLoop, calls=%fused_computation.67 | loop fusion | flops 532480 | bytes 164740 | tf_op jit(solution)/shard_map/stack | solution.py:197
  194.6 21.0 %add_bitcast_fusion.10 = f32[1,1,64,128]{3,2,1,0:T(8,128)S(1)} fusion(f32[512,128]{1,0:T(8,128)S(1)} %fusion.134, f32[]{:T(128)} %bitcast.212, f32[]{:T(128)} %bitcast.211, f32[]{:T(128)} %bitcast.210, f32[]{:T(128)} %bitcast.209, f32[]{:T(128)} %bitcast.208, f32[]{:T(128)} %bitcast.207, f32[]{:T(128)} %bitcast.206, f32[]{:T(128)} %bitcast.205, ...), kind=kLoop, calls=%fused_computation.79 | loop fusion | flops 532480 | bytes 164740 | tf_op jit(solution)/shard_map/stack | solution.py:197
  215.6 20.8 %add_bitcast_fusion.5 = f32[1,1,64,128]{3,2,1,0:T(8,128)S(1)} fusion(f32[512,128]{1,0:T(8,128)S(1)} %fusion.134, f32[]{:T(128)} %bitcast.245, f32[]{:T(128)} %bitcast.244, f32[]{:T(128)} %bitcast.243, f32[]{:T(128)} %bitcast.242, f32[]{:T(128)} %bitcast.241, f32[]{:T(128)} %bitcast.240, f32[]{:T(128)} %bitcast.239, f32[]{:T(128)} %bitcast.238, f32[]{:T(128)} %bitcast.237, ...), kind=kLoop, calls=%fused_computation.66 | loop fusion | flops 532480 | bytes 164740 | tf_op jit(solution)/shard_map/stack | solution.py:197
  236.4 20.8 %add_bitcast_fusion.9 = f32[1,1,64,128]{3,2,1,0:T(8,128)S(1)} fusion(f32[512,128]{1,0:T(8,128)S(1)} %fusion.134, f32[]{:T(128)} %bitcast.245, f32[]{:T(128)} %bitcast.244, f32[]{:T(128)} %bitcast.243, f32[]{:T(128)} %bitcast.242, f32[]{:T(128)} %bitcast.241, f32[]{:T(128)} %bitcast.240, f32[]{:T(128)} %bitcast.239, f32[]{:T(128)} %bitcast.238, f32[]{:T(128)} %bitcast.237, ...), kind=kLoop, calls=%fused_computation.74 | loop fusion | flops 532480 | bytes 164740 | tf_op jit(solution)/shard_map/stack | solution.py:197
  257.2 20.8 %add_bitcast_fusion.4 = f32[1,1,64,128]{3,2,1,0:T(8,128)S(1)} fusion(f32[512,128]{1,0:T(8,128)S(1)} %fusion.134, f32[]{:T(128)} %bitcast.278, f32[]{:T(128)} %bitcast.277, f32[]{:T(128)} %bitcast.276, f32[]{:T(128)} %bitcast.275, f32[]{:T(128)} %bitcast.274, f32[]{:T(128)} %bitcast.273, f32[]{:T(128)} %bitcast.272, f32[]{:T(128)} %bitcast.271, f32[]{:T(128)} %bitcast.270, ...), kind=kLoop, calls=%fused_computation.65 | loop fusion | flops 532480 | bytes 164740 | tf_op jit(solution)/shard_map/stack | solution.py:197
  278.0 20.8 %add_bitcast_fusion.8 = f32[1,1,64,128]{3,2,1,0:T(8,128)S(1)} fusion(f32[512,128]{1,0:T(8,128)S(1)} %fusion.134, f32[]{:T(128)} %bitcast.278, f32[]{:T(128)} %bitcast.277, f32[]{:T(128)} %bitcast.276, f32[]{:T(128)} %bitcast.275, f32[]{:T(128)} %bitcast.274, f32[]{:T(128)} %bitcast.273, f32[]{:T(128)} %bitcast.272, f32[]{:T(128)} %bitcast.271, f32[]{:T(128)} %bitcast.270, ...), kind=kLoop, calls=%fused_computation.69 | loop fusion | flops 532480 | bytes 164740 | tf_op jit(solution)/shard_map/stack | solution.py:197
  298.8 20.5 %add_bitcast_fusion.15 = f32[1,1,64,128]{3,2,1,0:T(8,128)S(1)} fusion(f32[512,128]{1,0:T(8,128)S(1)} %fusion.134, f32[]{:T(128)} %bitcast.47, f32[]{:T(128)} %bitcast.46, f32[]{:T(128)} %bitcast.45, f32[]{:T(128)} %bitcast.44, f32[]{:T(128)} %bitcast.43, f32[]{:T(128)} %bitcast.42, f32[]{:T(128)} %bitcast.41, f32[]{:T(128)} %bitcast.40, f32[]{:T(128)} %bitcast.39, ...), kind=kLoop, calls=%fused_computation.92 | loop fusion | flops 532480 | bytes 164740 | tf_op jit(solution)/shard_map/stack | solution.py:197
  319.3 20.6 %add_bitcast_fusion.14 = f32[1,1,64,128]{3,2,1,0:T(8,128)S(1)} fusion(f32[512,128]{1,0:T(8,128)S(1)} %fusion.134, f32[]{:T(128)} %bitcast.80, f32[]{:T(128)} %bitcast.79, f32[]{:T(128)} %bitcast.78, f32[]{:T(128)} %bitcast.77, f32[]{:T(128)} %bitcast.76, f32[]{:T(128)} %bitcast.75, f32[]{:T(128)} %bitcast.74, f32[]{:T(128)} %bitcast.73, f32[]{:T(128)} %bitcast.72, ...), kind=kLoop, calls=%fused_computation.91 | loop fusion | flops 532480 | bytes 164740 | tf_op jit(solution)/shard_map/stack | solution.py:197
  339.9 20.5 %add_bitcast_fusion.13 = f32[1,1,64,128]{3,2,1,0:T(8,128)S(1)} fusion(f32[512,128]{1,0:T(8,128)S(1)} %fusion.134, f32[]{:T(128)} %bitcast.113, f32[]{:T(128)} %bitcast.112, f32[]{:T(128)} %bitcast.111, f32[]{:T(128)} %bitcast.110, f32[]{:T(128)} %bitcast.109, f32[]{:T(128)} %bitcast.108, f32[]{:T(128)} %bitcast.107, f32[]{:T(128)} %bitcast.106, ...), kind=kLoop, calls=%fused_computation.90 | loop fusion | flops 532480 | bytes 164740 | tf_op jit(solution)/shard_map/stack | solution.py:197
  360.5 20.7 %add_bitcast_fusion.12 = f32[1,1,64,128]{3,2,1,0:T(8,128)S(1)} fusion(f32[512,128]{1,0:T(8,128)S(1)} %fusion.134, f32[]{:T(128)} %bitcast.146, f32[]{:T(128)} %bitcast.145, f32[]{:T(128)} %bitcast.144, f32[]{:T(128)} %bitcast.143, f32[]{:T(128)} %bitcast.142, f32[]{:T(128)} %bitcast.141, f32[]{:T(128)} %bitcast.140, f32[]{:T(128)} %bitcast.139, ...), kind=kLoop, calls=%fused_computation.89 | loop fusion | flops 532480 | bytes 164740 | tf_op jit(solution)/shard_map/stack | solution.py:197
  381.2 20.7 %add_bitcast_fusion.3 = f32[1,1,64,128]{3,2,1,0:T(8,128)S(1)} fusion(f32[512,128]{1,0:T(8,128)S(1)} %fusion.134, f32[]{:T(128)} %bitcast.315, f32[]{:T(128)} %bitcast.314, f32[]{:T(128)} %bitcast.313, f32[]{:T(128)} %bitcast.312, f32[]{:T(128)} %bitcast.311, f32[]{:T(128)} %bitcast.310, f32[]{:T(128)} %bitcast.309, f32[]{:T(128)} %bitcast.308, f32[]{:T(128)} %bitcast.307, ...), kind=kLoop, calls=%fused_computation.64 | loop fusion | flops 532480 | bytes 164740 | tf_op jit(solution)/shard_map/stack | solution.py:197
  401.9 20.7 %add_bitcast_fusion.2 = f32[1,1,64,128]{3,2,1,0:T(8,128)S(1)} fusion(f32[512,128]{1,0:T(8,128)S(1)} %fusion.134, f32[]{:T(128)} %bitcast.348, f32[]{:T(128)} %bitcast.347, f32[]{:T(128)} %bitcast.346, f32[]{:T(128)} %bitcast.345, f32[]{:T(128)} %bitcast.344, f32[]{:T(128)} %bitcast.343, f32[]{:T(128)} %bitcast.342, f32[]{:T(128)} %bitcast.341, f32[]{:T(128)} %bitcast.340, ...), kind=kLoop, calls=%fused_computation.63 | loop fusion | flops 532480 | bytes 164740 | tf_op jit(solution)/shard_map/stack | solution.py:197
  422.7 20.6 %add_bitcast_fusion.1 = f32[1,1,64,128]{3,2,1,0:T(8,128)S(1)} fusion(f32[512,128]{1,0:T(8,128)S(1)} %fusion.134, f32[]{:T(128)} %bitcast.381, f32[]{:T(128)} %bitcast.380, f32[]{:T(128)} %bitcast.379, f32[]{:T(128)} %bitcast.378, f32[]{:T(128)} %bitcast.377, f32[]{:T(128)} %bitcast.376, f32[]{:T(128)} %bitcast.375, f32[]{:T(128)} %bitcast.374, f32[]{:T(128)} %bitcast.373, ...), kind=kLoop, calls=%fused_computation.62 | loop fusion | flops 532480 | bytes 164740 | tf_op jit(solution)/shard_map/stack | solution.py:197
  443.3 21.0 %add_bitcast_fusion = f32[1,1,64,128]{3,2,1,0:T(8,128)S(1)} fusion(f32[512,128]{1,0:T(8,128)S(1)} %fusion.134, f32[]{:T(128)} %bitcast.414, f32[]{:T(128)} %bitcast.413, f32[]{:T(128)} %bitcast.412, f32[]{:T(128)} %bitcast.411, f32[]{:T(128)} %bitcast.410, f32[]{:T(128)} %bitcast.409, f32[]{:T(128)} %bitcast.408, f32[]{:T(128)} %bitcast.407, f32[]{:T(128)} %bitcast.406, ...), kind=kLoop, calls=%fused_computation.61 | loop fusion | flops 532480 | bytes 164740 | tf_op jit(solution)/shard_map/stack | solution.py:197
  471.7 19.7 %all-to-all-done.2 = f32[32,16,128]{2,1,0:T(8,128)S(1)} async-done(((f32[32,16,128]{2,1,0:T(8,128)}), f32[32,16,128]{2,1,0:T(8,128)S(1)}, u32[]{:S(2)}, u32[]{:S(2)}) %all-to-all-start.2) | async-done | bytes 262176 | tf_op jit(solution)/shard_map/all_to_all | solution.py:201
  492.9 8.5 %all-to-all-start.3 = ((f32[16,2,16,256]{3,2,1,0:T(8,128)}), f32[16,2,16,256]{3,2,1,0:T(8,128)S(1)}, u32[]{:S(2)}, u32[]{:S(2)}) async-start(f32[16,2,16,256]{3,2,1,0:T(8,128)} %bitcast.421), calls=%async_computation.3 | async-start | bytes 1048576 | tf_op jit(solution)/shard_map/all_to_all | solution.py:206
  (155 shorter events, 89.2 us)
Async XLA Ops:
  1.6 74.4 %collective-permute-start.1 = (f32[2,2,1,32,256]{4,3,2,1,0:T(8,128)S(1)}, f32[2,2,1,32,256]{4,3,2,1,0:T(8,128)S(1)}, u32[]{:S(2)}, u32[]{:S(2)}) collective-permute-start(f32[2,2,1,32,256]{4,3,2,1,0:T(8,128)S(1)} %get-tuple-element.118), channel_id=1, source_target_pairs={{1,0},{2,1},{3,2},{4,3},{5,4},{6,5},{7,6},{8,7},{9,8},{10,9},{11,1... | collective-permute-start | bytes 393224 | tf_op jit(solution)/shard_map/ppermute | solution.py:142
  2.9 73.1 %collective-permute-start.2 = (f32[2,2,1,32,256]{4,3,2,1,0:T(8,128)S(1)}, f32[2,2,1,32,256]{4,3,2,1,0:T(8,128)S(1)}, u32[]{:S(2)}, u32[]{:S(2)}) collective-permute-start(f32[2,2,1,32,256]{4,3,2,1,0:T(8,128)S(1)} %get-tuple-element.119), channel_id=1, source_target_pairs={{0,1},{1,2},{2,3},{3,4},{4,5},{5,6},{6,7},{7,8},{8,9},{9,10},{10,1... | collective-permute-start | bytes 393224 | tf_op jit(solution)/shard_map/ppermute | solution.py:141
  8.0 0.7 copy-start.12
  8.0 0.7 copy-start.10
  8.7 0.7 copy-start.11
  65.5 8.1 %copy-start = (f32[2,2,2,32,256]{4,3,2,1,0:T(8,128)S(1)}, f32[2,2,2,32,256]{4,3,2,1,0:T(8,128)}, u32[]{:S(2)}) copy-start(f32[2,2,2,32,256]{4,3,2,1,0:T(8,128)} %param.21) | copy-start | bytes 786436
  65.5 8.1 %copy-start.1 = (f32[256,256]{1,0:T(8,128)S(1)}, f32[256,256]{1,0:T(8,128)}, u32[]{:S(2)}) copy-start(f32[256,256]{1,0:T(8,128)} %constant.232.clone) | copy-start | bytes 786436
  73.6 1.0 copy-start.2
  76.0 0.8 copy-start.8
  78.6 14.4 %all-to-all-start = ((f32[16,2,16,256]{3,2,1,0:T(8,128)}), f32[16,2,16,256]{3,2,1,0:T(8,128)S(1)}, u32[]{:S(2)}, u32[]{:S(2)}) async-start(f32[16,2,16,256]{3,2,1,0:T(8,128)} %pad_maximum_fusion), calls=%async_computation | async-start | bytes 1048576 | tf_op jit(solution)/shard_map/all_to_all | solution.py:154
  83.3 3.4 copy-start.14
  86.7 6.3 %copy-start.6 = (f32[256,256]{1,0:T(8,128)S(1)}, f32[256,256]{1,0:T(8,128)}, u32[]{:S(2)}) copy-start(f32[256,256]{1,0:T(8,128)} %constant.236.clone) | copy-start | bytes 786436
  86.7 6.3 %copy-start.7 = (f32[256,256]{1,0:T(8,128)S(1)}, f32[256,256]{1,0:T(8,128)}, u32[]{:S(2)}) copy-start(f32[256,256]{1,0:T(8,128)} %constant.235.clone) | copy-start | bytes 786436
  93.1 1.0 copy-start.4
  94.4 36.3 %copy-start.3 = (f32[512,512]{1,0:T(8,128)S(1)}, f32[512,512]{1,0:T(8,128)}, u32[]{:S(2)}) copy-start(f32[512,512]{1,0:T(8,128)} %constant.238.clone) | copy-start | bytes 3145732
  95.3 35.4 %all-to-all-start.1 = ((f32[32,16,128]{2,1,0:T(8,128)}), f32[32,16,128]{2,1,0:T(8,128)S(1)}, u32[]{:S(2)}, u32[]{:S(2)}) async-start(f32[32,16,128]{2,1,0:T(8,128)} %bitcast.22), calls=%async_computation.1 | async-start | bytes 524288 | tf_op jit(solution)/shard_map/all_to_all | solution.py:167
  466.8 4.7 copy-start.5
  466.8 24.5 %all-to-all-start.2 = ((f32[32,16,128]{2,1,0:T(8,128)}), f32[32,16,128]{2,1,0:T(8,128)S(1)}, u32[]{:S(2)}, u32[]{:S(2)}) async-start(f32[32,16,128]{2,1,0:T(8,128)} %bitcast.417), calls=%async_computation.2 | async-start | bytes 524288 | tf_op jit(solution)/shard_map/all_to_all | solution.py:201
  492.9 18.2 %all-to-all-start.3 = ((f32[16,2,16,256]{3,2,1,0:T(8,128)}), f32[16,2,16,256]{3,2,1,0:T(8,128)S(1)}, u32[]{:S(2)}, u32[]{:S(2)}) async-start(f32[16,2,16,256]{3,2,1,0:T(8,128)} %bitcast.421), calls=%async_computation.3 | async-start | bytes 1048576 | tf_op jit(solution)/shard_map/all_to_all | solution.py:206
  501.4 13.6 %collective-permute-start = (f32[2,2,2,32,256]{4,3,2,1,0:T(8,128)S(1)}, f32[2,2,2,32,256]{4,3,2,1,0:T(8,128)S(1)}, u32[]{:S(2)}, u32[]{:S(2)}) collective-permute-start(f32[2,2,2,32,256]{4,3,2,1,0:T(8,128)S(1)} %copy-done), channel_id=1, source_target_pairs={{0,32},{32,0},{1,33},{33,1},{2,34},{34,2},{3,35},{35,3},{4,36},{36... | collective-permute-start | bytes 786440 | tf_op jit(solution)/shard_map/ppermute | solution.py:210
  515.2 4.3 copy-start.15
  515.6 9.8 %collective-permute-start.3 = (f32[2,32,256]{2,1,0:T(8,128)S(1)}, f32[2,32,256]{2,1,0:T(8,128)S(1)}, u32[]{:S(2)}, u32[]{:S(2)}) collective-permute-start(f32[2,32,256]{2,1,0:T(8,128)S(1)} %get-tuple-element.108), channel_id=1, source_target_pairs={{0,64},{64,128},{128,192},{192,256},{256,320},{320,384},{384,448},... | collective-permute-start | bytes 196616 | tf_op jit(solution)/shard_map/ppermute | solution.py:222
  520.9 4.5 collective-permute-start.4
  523.1 6.4 %collective-permute-start.5 = (f32[2,2,1,32,256]{4,1,3,2,0:T(2,128)S(1)}, f32[2,2,1,32,256]{4,1,3,2,0:T(2,128)S(1)}, u32[]{:S(2)}, u32[]{:S(2)}) collective-permute-start(f32[2,2,1,32,256]{4,1,3,2,0:T(2,128)S(1)} %get-tuple-element.115), channel_id=1, source_target_pairs={{1,0},{2,1},{3,2},{4,3},{5,4},{6,5},{7,6},{8,7},{9,8},{10,9},{11,1... | collective-permute-start | bytes 393224 | tf_op jit(solution)/shard_map/ppermute | solution.py:220
  (5 other events, 3.3 us)

commit v2 on v1

v2 whole, which is shorter than its diff:
```python
import math

import jax
import jax.numpy as jnp
import numpy as np
from jax import lax
from jax.experimental import pallas as pl
from jax.experimental.pallas import tpu as pltpu
from jax.sharding import PartitionSpec as P

STEPS = 16
NODES = 4
SWEEPS = 8
GX = 32
GY = 256
NZ = 64

DIFFUSION = 0.5
REACTION = 1.0
HIGH = lax.Precision.HIGHEST


def legendre_pair(degree, point):
    previous_term, current_term = (1.0, point)
    for degree_now in range(1, degree):
        previous_term, current_term = (
            current_term,
            ((2 * degree_now + 1) * point * current_term - degree_now * previous_term)
            / (degree_now + 1),
        )
    return (current_term, previous_term)


def radau_value(count, point):
    high_term, low_term = legendre_pair(count, point)
    return high_term - low_term


def radau_points(count):
    roots_found = []
    samples = 4000
    for sample_index in range(samples):
        left_end = -1.0 + 2.0 * sample_index / samples
        right_end = -1.0 + 2.0 * (sample_index + 1) / samples
        if radau_value(count, left_end) * radau_value(count, right_end) < 0.0:
            for halving in range(200):
                middle = 0.5 * (left_end + right_end)
                if radau_value(count, left_end) * radau_value(count, middle) <= 0.0:
                    right_end = middle
                else:
                    left_end = middle
            roots_found.append(0.5 * (left_end + right_end))
    roots_found.append(1.0)
    return [(root_value + 1.0) / 2.0 for root_value in roots_found]


def collocation_matrix(node_count):
    points = radau_points(node_count)
    node_table = [[0.0] * node_count for row_number in range(node_count)]
    for column in range(node_count):
        coeffs = [1.0]
        for another in range(node_count):
            if another != column:
                spacing = points[column] - points[another]
                raised = [0.0] + coeffs
                lowered = [entry * points[another] for entry in coeffs] + [0.0]
                coeffs = [
                    (first_entry - second_entry) / spacing
                    for first_entry, second_entry in zip(raised, lowered)
                ]
        integral = [0.0] + [
            entry / (exponent_index + 1) for exponent_index, entry in enumerate(coeffs)
        ]
        for row_number in range(node_count):
            running = 0.0
            for exponent_index in range(len(integral) - 1, -1, -1):
                running = running * points[row_number] + integral[exponent_index]
            node_table[row_number][column] = running
    return node_table


def sine_matrix(count):
    index = np.arange(1, count + 1)
    return math.sqrt(2.0 / (count + 1)) * np.sin(np.pi * np.outer(index, index) / (count + 1))


def eigenvalues(count):
    return 2.0 * np.cos(np.pi * np.arange(1, count + 1) / (count + 1))


def tables():
    coll = np.array(collocation_matrix(NODES))
    sx, sy, sz = (sine_matrix(n) for n in (GX, GY, NZ))
    kx = np.einsum("kx,fg->kfgx", sx, np.eye(8)).reshape(256, 256)
    n = np.arange(STEPS)
    real_dft = np.zeros((8, 2, STEPS))
    for q in range(8):
        real_dft[q, 0] = np.cos(2 * np.pi * q * n / STEPS)
        real_dft[q, 1] = -np.sin(2 * np.pi * q * n / STEPS) if q else np.cos(np.pi * n)
    shifted = np.zeros_like(real_dft)
    shifted[:, :, :-1] = real_dft[:, :, 1:]
    split = real_dft.reshape(8, 2, 8, 2)
    shifted = shifted.reshape(8, 2, 8, 2)
    nodes = np.eye(NODES).reshape(NODES, 2, 2)
    last = np.zeros((NODES, 2, 2))
    last[:, 1, 1] = 1.0
    two = np.eye(2)
    form = "qrsn,mtj,kl,zw->qkrmzstlnjw"
    mu0 = -np.einsum(form, split, nodes, two, two).reshape(256, 256)
    mu1 = np.einsum(form, shifted, last, two, two).reshape(256, 256)
    mf = np.einsum(form, split, coll.reshape(NODES, 2, 2), two, two).reshape(256, 256)
    mi = np.einsum("qrsn,mtj,kl,zw->stlnjwqkrmz", split, nodes, two, two).reshape(256, 256)
    zf = np.einsum("rp,mn,ksz->rmkspnz", two, np.eye(4), sz.reshape(NZ, 32, 2)).reshape(512, 512)
    lam_z, lam_x, lam_y = (eigenvalues(n) for n in (NZ, GX, GY))
    lam_xy = np.repeat(lam_x, 8)[:, None] + lam_y[None]
    lam_zy = lam_z[None, :, None] + lam_y.reshape(2, 1, 128)
    lam_x = np.broadcast_to(lam_x[:, None, None], (GX, 8, 128))
    start = np.linalg.solve(coll, np.ones(NODES))
    arrays = dict(sy=sy, kx=kx, lam_xy=lam_xy, mu0=mu0, mu1=mu1, mf=mf, zf=zf, zt=zf.T, mi=mi,
                  kt=kx.T, lam_zy=lam_zy, lam_x=lam_x)
    return coll, start, {k: np.asarray(v, np.float32) for k, v in arrays.items()}


COLL, START, TABLES = tables()
NAMES = tuple(TABLES)


def dot(a, b):
    return jnp.dot(a, b, precision=HIGH, preferred_element_type=jnp.float32)


def horner_tables(q, params, coef, tab, lam):
    partner = (16 - q) % 16 + 8 * ((8 - q) // 8)
    own = params[2 * (q // 2)] + params[2 * (q // 2) + 1]
    mate = params[2 * (partner // 2)] + params[2 * (partner // 2) + 1]
    row = lax.broadcasted_iota(jnp.int32, (8, 128), 0)
    odd = q % 2 == 1
    own = jnp.where(odd, pltpu.roll(own, 4, 0), own)
    mate = jnp.where(odd, mate, pltpu.roll(mate, 4, 0))
    x = jnp.where(row < 4, own, mate)
    bre, bim, mre, mim, dre, dim = [x if c == 0 else pltpu.roll(x, 128 - 16 * c, 1) for c in range(6)]
    pre, pim = bre * mre - bim * mim, bre * mim + bim * mre
    scale = 6.0 * DIFFUSION - REACTION
    ere, eim = 1.0 + scale * dre, scale * dim
    mag = ere * ere + eim * eim
    gre, gim = ere / mag, -eim / mag
    are, aim = DIFFUSION * dre, DIFFUSION * dim
    rre, rim = are * gre - aim * gim, are * gim + aim * gre
    first = q == 0
    for power in range(SWEEPS):
        tre, tim = pre * gre - pim * gim, pre * gim + pim * gre
        gre, gim = gre * rre - gim * rim, gre * rim + gim * rre
        kre, kim = (jnp.sum(v[0:4], axis=0, keepdims=True) for v in (tre, tim))
        ore, oim = (jnp.sum(v[4:8], axis=0, keepdims=True) for v in (tre, tim))
        both = kre + ore
        coef[0, power : power + 1, :] = jnp.where(first, kre, both)
        coef[1, power : power + 1, :] = jnp.where(first, 0.0, kim - oim)
        coef[2, power : power + 1, :] = jnp.where(first, ore, both)

    def entry(e, carry):
        following = []
        for a, c in enumerate(carry):
            col = jnp.broadcast_to(c[:, 0:1], (8, 128))
            acc = jnp.broadcast_to(col[SWEEPS - 1 : SWEEPS], (64, 128))
            for power in range(SWEEPS - 2, -1, -1):
                acc = acc * lam + col[power : power + 1]
            tab[a, e] = acc
            following.append(pltpu.roll(c, 127, 1))
        return tuple(following)

    lax.fori_loop(0, 16, entry, (coef[0], coef[1], coef[2]))


def pack_params(node, mix, back, shifts, out):
    row = lax.broadcasted_iota(jnp.int32, (8, 128), 0)
    lane = lax.broadcasted_iota(jnp.int32, (8, 128), 1)
    kind, i, j = lane // 16, (lane // 4) % 4, lane % 4
    k, m = row // 4, row % 4
    acc = jnp.zeros((8, 128), jnp.float32)
    for c in range(2):
        for kk in range(2):
            here = k == kk
            for l in range(2):
                mine = 2 * node + l
                at_mix = here & (kind == 2 + c) & (m == mine)
                at_back = here & (kind == c) & (i == mine)
                for n in range(4):
                    acc = jnp.where(at_mix & (j == n), mix[c, kk, l, n], acc)
                    acc = jnp.where(at_back & (m == n), back[c, kk, l, n], acc)
                acc = jnp.where(here & (kind == 4 + c) & (m == mine), shifts[c, kk, l], acc)
    out[...] = acc


def kernel(u_ref, init_ref, alpha_ref, mix_ref, back_ref, shifts_ref, *refs):
    consts = dict(zip(NAMES, refs[: len(NAMES)]))
    refs = refs[len(NAMES) :]
    out_u, out_r = refs[:2]
    refs = refs[2:]
    held = dict(zip(NAMES, refs[: len(NAMES)]))
    refs = refs[len(NAMES) :]
    (su, ru, sf, rf, sp, rp, s2, r2, s3, r3, s4, r4, halo, grid, ub, wb, whalo, before, coef, tab,
     sw, ow, load_sem, send_sem, recv_sem) = refs
    step, node, space = (lax.axis_index(a) for a in ("step", "node", "space"))
    me = step * 2 + node

    loads = {}
    for index, name in enumerate(NAMES):
        loads[name] = pltpu.make_async_copy(consts[name], held[name], load_sem.at[index])
        loads[name].start()

    def get(name):
        loads[name].wait()
        return held[name]

    barrier = pltpu.get_barrier_semaphore()

    def group_id(d):
        other = (me + d) % 16
        return other, {"step": other // 2, "node": other % 2}

    def greet_group(d, _):
        pl.semaphore_signal(barrier, inc=1, device_id=group_id(d)[1])
        return 0

    def greet_space(d, _):
        pl.semaphore_signal(barrier, inc=1, device_id={"space": (space + d) % 32})
        return 0

    lax.fori_loop(1, 16, greet_group, 0)
    lax.fori_loop(1, 32, greet_space, 0)
    pl.semaphore_wait(barrier, 46)

    def remote(src, dst, sem, device):
        return pltpu.make_async_remote_copy(
            src_ref=src, dst_ref=dst, send_sem=send_sem.at[sem], recv_sem=recv_sem.at[sem], device_id=device
        )

    up, down = {"space": (space + 1) % 32}, {"space": (space + 31) % 32}
    HALO_UP, HALO_DOWN, GROUP_U, GROUP_F, PARAMS, SPACE, BACK, CORR, OTHER, W_UP, W_DOWN, BEFORE = range(12)
    pending = [
        remote(u_ref.at[:, 1], halo.at[0], HALO_UP, up),
        remote(u_ref.at[:, 0], halo.at[1], HALO_DOWN, down),
    ]
    for copy in pending:
        copy.start()

    def to_group(src, dst, sem):
        def body(d, _):
            other, device = group_id(d)
            remote(src.at[other], dst.at[me], sem, device).start()
            return 0
        lax.fori_loop(1, 16, body, 0)
        dst[me] = src[me]

    def to_space(src, dst, sem):
        def body(d, _):
            other = (space + d) % 32
            remote(src.at[other], dst.at[space], sem, {"space": other}).start()
            return 0
        lax.fori_loop(1, 32, body, 0)
        dst[space] = src[space]

    def arrived(ref, sem, count):
        part = ref.at[pl.ds(0, count)]
        remote(part, part, sem, up).wait_recv()

    def sent(ref, sem, count):
        part = ref.at[pl.ds(0, count)]
        remote(part, part, sem, up).wait_send()

    sy, kx = get("sy"), get("kx")
    uh = dot(kx[...], dot(u_ref[...].reshape(256, 256), sy[...]))
    su[...] = uh.reshape(16, 16, 256)
    to_group(su, ru, GROUP_U)

    low = jnp.where(space == 0, 0.0, DIFFUSION)
    high = jnp.where(space == 31, 0.0, DIFFUSION)
    begin = [
        jnp.where(step == 0, jnp.where(node == 0, START[m], START[2 + m]), 0.0).astype(jnp.float32) for m in range(2)
    ]
    pending[0].wait_recv()
    pending[1].wait_recv()
    for nm in range(4):
        for z in range(2):
            u = u_ref[nm, z]
            beside = DIFFUSION * u_ref[nm, 1 - z] + (low if z == 0 else high) * halo[z, nm]
            value = beside - (6.0 * DIFFUSION - REACTION) * u - REACTION * (u * u * u)
            if nm < 2:
                value = value + begin[nm] * init_ref[z]
            grid[nm * 2 + z] = value
    fh = dot(kx[...], dot(grid[...].reshape(256, 256), sy[...]))
    fh = fh + DIFFUSION * get("lam_xy")[...] * su[...].reshape(256, 256)
    sf[...] = fh.reshape(16, 16, 256)
    to_group(sf, rf, GROUP_F)

    pack_params(node, mix_ref, back_ref, shifts_ref, sp)

    def send_params(d, _):
        remote(sp, rp.at[me], PARAMS, group_id(d)[1]).start()
        return 0

    lax.fori_loop(1, 16, send_params, 0)
    rp[me] = sp[...]

    rate = alpha_ref[0].astype(jnp.float32) * (math.log(2.0) / 16.0 / STEPS)
    col = lax.broadcasted_iota(jnp.int32, (1, 256), 1)
    when = (2 * (col // 32) + (col // 4) % 2).astype(jnp.float32)
    scale0, scale1 = jnp.exp(-rate * when), jnp.exp(-rate * (when + 1.0))
    mu = get("mu0")[...] * scale0 + get("mu1")[...] * scale1
    mf = get("mf")[...] * scale0
    arrived(ru, GROUP_U, 15)
    spec = dot(mu, ru[...].reshape(256, 256))
    arrived(rf, GROUP_F, 15)
    spec = spec + dot(mf, rf[...].reshape(256, 256))
    for h in range(2):
        s2[:, h] = spec[:, h * 128 : h * 128 + 128].reshape(16, 16, 128)
    s2_flat, r2_flat = s2.reshape(32, 16, 128), r2
    to_space(s2_flat, r2_flat, SPACE)
    other_u = remote(u_ref, ub.at[node], OTHER, {"node": 1 - node})
    other_u.start()
    ub[node] = u_ref[...]

    arrived(rp, PARAMS, 15)
    q = space // 4
    lam = get("lam_zy")[space % 2] + jnp.broadcast_to(
        get("lam_x")[2 * me + (space // 2) % 2][0:1], (64, 128))
    horner_tables(q, rp, coef, tab, lam)
    row = lax.broadcasted_iota(jnp.int32, (256, 256), 0)
    when = (2 * (row // 32) + (row // 4) % 2).astype(jnp.float32)
    held["mi"][...] = get("mi")[...] * (jnp.exp(rate * when) * (1.0 / STEPS))

    zf, zt = get("zf"), get("zt")
    arrived(r2_flat, SPACE, 31)
    sw[...] = dot(zf[...], r2[...].reshape(512, 128)).reshape(8, 64, 128)

    def solve(z, _):
        at = pl.ds(pl.multiple_of(z * 8, 8), 8)
        s = [sw[i, at, :] for i in range(8)]
        for i in range(4):
            re = im = None
            for j in range(4):
                a, e, d = (tab[c, 4 * i + j, at, :] for c in range(3))
                tre, tim = a * s[j] - e * s[4 + j], e * s[j] + d * s[4 + j]
                re, im = (tre, tim) if re is None else (re + tre, im + tim)
            ow[i, at, :] = re
            ow[4 + i, at, :] = im
        return 0

    lax.fori_loop(0, 8, solve, 0)
    s3[...] = dot(zt[...], ow[...].reshape(512, 128)).reshape(32, 16, 128)
    to_space(s3, r3, BACK)
    kt = get("kt")
    arrived(r3, BACK, 31)
    for h in range(2):
        part = r3[...].reshape(16, 2, 16, 128)[:, h].reshape(256, 128)
        s4[:, :, :, h * 128 : h * 128 + 128] = dot(held["mi"][...], part).reshape(8, 2, 16, 128)

    def send_corr(d, _):
        other, device = group_id(d)
        remote(s4.at[other // 2], r4.at[:, me], CORR, device).start()
        return 0

    lax.fori_loop(1, 16, send_corr, 0)
    r4[:, me] = s4[step]
    other_u.wait_recv()
    whole = r4.at[:, pl.ds(0, 15)]
    remote(whole, whole, CORR, up).wait_recv()
    for g in range(2):
        d = dot(dot(kt[...], r4[g].reshape(256, 256)), sy[...])
        ub[g] = ub[g] + d.reshape(4, 2, 32, 256)
    out_u[...] = ub[node]

    weight = [
        [jnp.where(node == 0, COLL[m][j], COLL[2 + m][j]).astype(jnp.float32) for j in range(4)] for m in range(2)
    ]

    def nodes_at(n, z):
        return [ub[j // 2, 2 * n + j % 2, z] for j in range(4)]

    for n in range(2):
        for z in range(2):
            u = nodes_at(n, z)
            for m in range(2):
                wb[2 * n + m, z] = sum(weight[m][j] * u[j] for j in range(4))
    last = [
        remote(wb.at[:, 1], whalo.at[0], W_UP, up),
        remote(wb.at[:, 0], whalo.at[1], W_DOWN, down),
        remote(ub.at[1, 3], before, BEFORE, {"step": (step + 1) % 8}),
    ]
    for copy in last:
        copy.start()
    x = lax.broadcasted_iota(jnp.int32, (32, 256), 0)
    y = lax.broadcasted_iota(jnp.int32, (32, 256), 1)
    for n in range(2):
        for z in range(2):
            cubes = [v * v * v for v in nodes_at(n, z)]
            for m in range(2):
                w = wb[2 * n + m, z]
                beside = (
                    wb[2 * n + m, 1 - z]
                    + jnp.where(x == 0, 0.0, pltpu.roll(w, 1, 0))
                    + jnp.where(x == 31, 0.0, pltpu.roll(w, 31, 0))
                    + jnp.where(y == 0, 0.0, pltpu.roll(w, 1, 1))
                    + jnp.where(y == 255, 0.0, pltpu.roll(w, 255, 1))
                )
                value = DIFFUSION * beside - (6.0 * DIFFUSION - REACTION) * w
                value = value - REACTION * sum(weight[m][j] * cubes[j] for j in range(4)) - ub[node, 2 * n + m, z]
                if n == 1:
                    value = value + ub[1, 1, z]
                out_r[2 * n + m, z] = value
    for copy in last:
        copy.wait_recv()
    for z in range(2):
        opening = jnp.where(step == 0, init_ref[z], before[z])
        for nm in range(4):
            edge = (low if z == 0 else high) * whalo[z, nm]
            out_r[nm, z] = out_r[nm, z] + (edge + opening if nm < 2 else edge)

    for copy in pending + last + [other_u]:
        copy.wait_send()
    sent(su, GROUP_U, 15)
    sent(sf, GROUP_F, 15)
    sent(rp, PARAMS, 15)
    sent(s3, SPACE, 31)
    sent(s3, BACK, 31)
    remote(whole, whole, CORR, up).wait_send()


def on_device(iterate, initial_value, alpha_power, node_mix, node_back, shifts):
    consts = [jnp.asarray(TABLES[name]) for name in NAMES]
    f32 = jnp.float32
    vmem = lambda *shape: pltpu.VMEM(shape, f32)
    block = jax.ShapeDtypeStruct((4, 2, 32, 256), f32)
    in_vmem, in_smem = (pl.BlockSpec(memory_space=m) for m in (pltpu.VMEM, pltpu.SMEM))
    updated, residual = pl.pallas_call(
        kernel,
        out_shape=(block, block),
        in_specs=[in_vmem, in_vmem] + [in_smem] * 4 + [pl.BlockSpec(memory_space=pl.ANY)] * len(NAMES),
        out_specs=(in_vmem, in_vmem),
        scratch_shapes=[vmem(*TABLES[name].shape) for name in NAMES]
        + [vmem(16, 16, 256)] * 4
        + [vmem(8, 128), vmem(16, 8, 128)]
        + [vmem(16, 2, 16, 128), vmem(32, 16, 128)]
        + [vmem(32, 16, 128)] * 2
        + [vmem(8, 2, 16, 256), vmem(2, 16, 16, 256)]
        + [vmem(2, 4, 32, 256), vmem(8, 32, 256)]
        + [vmem(2, 4, 2, 32, 256), vmem(4, 2, 32, 256), vmem(2, 4, 32, 256), vmem(2, 32, 256)]
        + [vmem(3, 8, 128), vmem(3, 16, 64, 128)]
        + [vmem(8, 64, 128)] * 2
        + [pltpu.SemaphoreType.DMA((len(NAMES),)), pltpu.SemaphoreType.DMA((12,)), pltpu.SemaphoreType.DMA((12,))],
        compiler_params=pltpu.CompilerParams(
            collective_id=0, has_side_effects=True, vmem_limit_bytes=48 * 1024 * 1024
        ),
    )(iterate.reshape(4, 2, 32, 256), initial_value, alpha_power, node_mix, node_back, shifts, *consts)
    return updated.reshape(iterate.shape), residual.reshape(iterate.shape)


def solution(mesh):
    in_specs = (
        P("step", "node", "space", None, None),
        P("space", None, None),
        P(),
        P(None, "step", "node", None),
        P(None, "step", "node", None),
        P(None, "step", "node"),
    )
    out_specs = (P("step", "node", "space", None, None), P("step", "node", "space", None, None))
    return jax.shard_map(
        on_device, mesh=mesh, in_specs=in_specs, out_specs=out_specs, check_vma=False
    )
```

time: 537 us -> 101 us (0.19)
  other arithmetic: 335 us -> 0 us
  Pallas kernels: 0 us -> 82.9 us
  blocking collectives: 54.9 us -> 0 us
  waiting for transfers between devices: 52.8 us -> 0 us
  starting transfers between devices: 48.8 us -> 0 us
  matrix products: 11.7 us -> 0 us
  local copies, waits for them, and re-layouts: 26.9 us -> 16.4 us
    another operation x20 -> x0, other arithmetic: 333 us -> none  [the longest x16 332 us: apply(): jnp.stack([sum((horner(c[:, i, j]) * v[j] for j in range(4))) for i in ra...]
    pallas_call x0 -> x1, Pallas kernels: none -> 82.9 us  [on_device(): pl.pallas_call(kernel, out_shape=(block, block), in_specs=[in_vmem, in_vm...]
    all_gather x6 -> x0, blocking collectives: 54.9 us -> none  [the longest x3 45.4 us: on_device(): lax.all_gather(x, 'step', axis=1, tiled=True)]
    all_to_all x4 -> x0, waiting for transfers between devices: 47.4 us -> none  [the longest x1 19.7 us: on_device(): back = lax.all_to_all(back, 'space', 0, 0, tiled=True)]
    all_to_all x4 -> x0, starting transfers between devices: 31.6 us -> none  [the longest x1 13.7 us: on_device(): spec = lax.all_to_all(spec, 'space', 0, 0, tiled=True).reshape(512, 128)]
    ppermute x6 -> x0, starting transfers between devices: 17.2 us -> none  [the longest x1 5.01 us: on_device(): below = lax.ppermute(iterate[:, :, 1:], 'space', ring_up)]
    slice x28 -> x0, local copies, waits for them, and re-layouts: 16.2 us -> none  [the longest x18 12.9 us: horner(): acc = acc * lam + c[j]]
    dot_general x15 -> x0, matrix products: 11.7 us -> none  [the longest x13 8.81 us: dot(): return jnp.dot(a, b, precision=HIGH, preferred_element_type=jnp.float32)]
  transfers between devices with their start and end apart: 10 -> 0, of which waited for: 6 -> 0; matrix products, arithmetic and copies ran while one was open for 4% -> 0% of each run, Pallas kernels for 0% -> 0%
where the time goes in v2:
time: 101 us
  Pallas kernels  82.9 us (82%)
  local copies, waits for them, and re-layouts  16.4 us (16%)
  between operations  1.33 us (1%)
    pallas_call x1, Pallas kernels, on_device(): pl.pallas_call(kernel, out_shape=(block, block), in_specs=[in_vmem, in_vm...  82.9 us
    unnamed x36, local copies, waits for them, and re-layouts  16.4 us

profile of v2, /device:TPU:1, one launch (start us, length us, event | category | flops | bytes accessed | tf_op | source)
XLA Modules:
  0.0 100.6 jit_solution(4233040214516990122)
XLA Ops:
  0.6 0.0 copy-start.16
  1.3 0.0 copy-done.16
  1.3 0.0 copy-start
  1.3 1.2 %copy-done = f32[512,512]{1,0:T(8,128)S(1)} copy-done((f32[512,512]{1,0:T(8,128)S(1)}, f32[512,512]{1,0:T(8,128)}, u32[]{:S(2)}) %copy-start) | copy-done | bytes 1048600
  2.5 0.0 copy-start.1
  2.5 1.2 %copy-done.1 = f32[512,512]{1,0:T(8,128)S(1)} copy-done((f32[512,512]{1,0:T(8,128)S(1)}, f32[512,512]{1,0:T(8,128)}, u32[]{:S(2)}) %copy-start.1) | copy-done | bytes 1048600
  3.8 0.9 copy-done.2
  4.7 0.0 copy-start.3
  4.7 0.9 copy-done.3
  5.7 0.9 copy-done.4
  6.6 0.9 copy-done.5
  7.6 0.9 copy-done.6
  8.5 0.9 copy-done.7
  9.5 0.9 copy-done.8
  10.4 0.9 copy-done.9
  11.4 0.9 copy-done.10
  12.3 0.9 copy-done.11
  13.2 0.8 copy-done.12
  14.1 0.8 copy-done.13
  14.9 0.7 copy-done.14
  15.6 0.7 copy-done.15
  16.3 82.9 %shard_map.185 = (f32[4,2,32,256]{3,2,1,0:T(8,128)S(1)}, f32[4,2,32,256]{3,2,1,0:T(8,128)S(1)}) custom-call(f32[4,2,32,256]{3,2,1,0:T(8,128)S(1)} %bitcast.3, f32[2,32,256]{2,1,0:T(8,128)S(1)} %copy-done.12, s32[1]{0:T(128)S(6)} %copy.22.alpha_ref, f32[2,2,2,4]{3,2,1,0:T(2,128)S(1)} %copy-done.14, f32[2,2,2,4]{3,2,1,0:T(2,128)S(1)} %copy-done.15, ...), custom_call_target="tpu_custom_call" | custom-call | tf_op jit(solution)/shard_map/pallas_call | solution.py:435
  99.2 0.7 copy.23
  99.9 0.7 copy.24
  (13 shorter events, 0.0 us)
Async XLA Ops:
  0.6 0.7 copy-start.16
  1.3 1.2 %copy-start = (f32[512,512]{1,0:T(8,128)S(1)}, f32[512,512]{1,0:T(8,128)}, u32[]{:S(2)}) copy-start(f32[512,512]{1,0:T(8,128)} %constant.31.clone.refs_7_) | copy-start | bytes 3145732
  2.5 1.2 %copy-start.1 = (f32[512,512]{1,0:T(8,128)S(1)}, f32[512,512]{1,0:T(8,128)}, u32[]{:S(2)}) copy-start(f32[512,512]{1,0:T(8,128)} %constant.30.clone.refs_6_) | copy-start | bytes 3145732
  3.8 0.9 copy-start.2
  4.7 0.9 copy-start.3
  5.7 0.9 copy-start.4
  6.6 0.9 copy-start.5
  7.6 0.9 copy-start.6
  8.5 0.9 copy-start.7
  9.5 0.9 copy-start.8
  10.4 0.9 copy-start.9
  11.4 0.9 copy-start.10
  12.3 0.9 copy-start.11
  13.2 0.8 copy-start.12
  14.1 0.8 copy-start.13
  14.9 0.7 copy-start.14
  15.6 0.7 copy-start.15

commit v3 on v2

--- a/solution.py
+++ b/solution.py
@@ -191,22 +191,26 @@
     out[...] = acc
 
 
-def kernel(u_ref, init_ref, alpha_ref, mix_ref, back_ref, shifts_ref, *refs):
+def kernel(u_hbm, init_hbm, alpha_ref, mix_ref, back_ref, shifts_ref, *refs):
     consts = dict(zip(NAMES, refs[: len(NAMES)]))
     refs = refs[len(NAMES) :]
     out_u, out_r = refs[:2]
     refs = refs[2:]
     held = dict(zip(NAMES, refs[: len(NAMES)]))
     refs = refs[len(NAMES) :]
-    (su, ru, sf, rf, sp, rp, s2, r2, s3, r3, s4, r4, halo, grid, ub, wb, whalo, before, coef, tab,
+    (u_ref, init_ref, su, ru, sf, rf, sp, rp, s2, r2, s3, r3, s4, r4, halo, grid, ub, wb, whalo, before, coef, tab,
      sw, ow, load_sem, send_sem, recv_sem) = refs
     step, node, space = (lax.axis_index(a) for a in ("step", "node", "space"))
     me = step * 2 + node
 
+    load_u = pltpu.make_async_copy(u_hbm, u_ref, load_sem.at[len(NAMES)])
+    load_init = pltpu.make_async_copy(init_hbm, init_ref, load_sem.at[len(NAMES) + 1])
+    load_u.start()
     loads = {}
     for index, name in enumerate(NAMES):
         loads[name] = pltpu.make_async_copy(consts[name], held[name], load_sem.at[index])
         loads[name].start()
+    load_init.start()
 
     def get(name):
         loads[name].wait()
@@ -238,8 +242,8 @@
     up, down = {"space": (space + 1) % 32}, {"space": (space + 31) % 32}
     HALO_UP, HALO_DOWN, GROUP_U, GROUP_F, PARAMS, SPACE, BACK, CORR, OTHER, W_UP, W_DOWN, BEFORE = range(12)
     pending = [
-        remote(u_ref.at[:, 1], halo.at[0], HALO_UP, up),
-        remote(u_ref.at[:, 0], halo.at[1], HALO_DOWN, down),
+        remote(u_hbm.at[:, 1], halo.at[0], HALO_UP, up),
+        remote(u_hbm.at[:, 0], halo.at[1], HALO_DOWN, down),
     ]
     for copy in pending:
         copy.start()
@@ -268,6 +272,7 @@
         part = ref.at[pl.ds(0, count)]
         remote(part, part, sem, up).wait_send()
 
+    load_u.wait()
     sy, kx = get("sy"), get("kx")
     uh = dot(kx[...], dot(u_ref[...].reshape(256, 256), sy[...]))
     su[...] = uh.reshape(16, 16, 256)
@@ -278,6 +283,7 @@
     begin = [
         jnp.where(step == 0, jnp.where(node == 0, START[m], START[2 + m]), 0.0).astype(jnp.float32) for m in range(2)
     ]
+    load_init.wait()
     pending[0].wait_recv()
     pending[1].wait_recv()
     for nm in range(4):
@@ -316,7 +322,7 @@
         s2[:, h] = spec[:, h * 128 : h * 128 + 128].reshape(16, 16, 128)
     s2_flat, r2_flat = s2.reshape(32, 16, 128), r2
     to_space(s2_flat, r2_flat, SPACE)
-    other_u = remote(u_ref, ub.at[node], OTHER, {"node": 1 - node})
+    other_u = remote(u_hbm, ub.at[node], OTHER, {"node": 1 - node})
     other_u.start()
     ub[node] = u_ref[...]
 
@@ -431,13 +437,14 @@
     f32 = jnp.float32
     vmem = lambda *shape: pltpu.VMEM(shape, f32)
     block = jax.ShapeDtypeStruct((4, 2, 32, 256), f32)
-    in_vmem, in_smem = (pl.BlockSpec(memory_space=m) for m in (pltpu.VMEM, pltpu.SMEM))
+    in_vmem, in_smem, in_any = (pl.BlockSpec(memory_space=m) for m in (pltpu.VMEM, pltpu.SMEM, pl.ANY))
     updated, residual = pl.pallas_call(
         kernel,
         out_shape=(block, block),
-        in_specs=[in_vmem, in_vmem] + [in_smem] * 4 + [pl.BlockSpec(memory_space=pl.ANY)] * len(NAMES),
+        in_specs=[in_any] * 2 + [in_smem] * 4 + [in_any] * len(NAMES),
         out_specs=(in_vmem, in_vmem),
         scratch_shapes=[vmem(*TABLES[name].shape) for name in NAMES]
+        + [vmem(4, 2, 32, 256), vmem(2, 32, 256)]
         + [vmem(16, 16, 256)] * 4
         + [vmem(8, 128), vmem(16, 8, 128)]
         + [vmem(16, 2, 16, 128), vmem(32, 16, 128)]
@@ -447,9 +454,9 @@
         + [vmem(2, 4, 2, 32, 256), vmem(4, 2, 32, 256), vmem(2, 4, 32, 256), vmem(2, 32, 256)]
         + [vmem(3, 8, 128), vmem(3, 16, 64, 128)]
         + [vmem(8, 64, 128)] * 2
-        + [pltpu.SemaphoreType.DMA((len(NAMES),)), pltpu.SemaphoreType.DMA((12,)), pltpu.SemaphoreType.DMA((12,))],
+        + [pltpu.SemaphoreType.DMA((len(NAMES) + 2,)), pltpu.SemaphoreType.DMA((12,)), pltpu.SemaphoreType.DMA((12,))],
         compiler_params=pltpu.CompilerParams(
-            collective_id=0, has_side_effects=True, vmem_limit_bytes=48 * 1024 * 1024
+            collective_id=0, has_side_effects=True, vmem_limit_bytes=63 * 1024 * 1024
         ),
     )(iterate.reshape(4, 2, 32, 256), initial_value, alpha_power, node_mix, node_back, shifts, *consts)
     return updated.reshape(iterate.shape), residual.reshape(iterate.shape)

time: 101 us -> 87.3 us (0.86)
  local copies, waits for them, and re-layouts: 16.4 us -> 2.42 us
    unnamed x36 -> x4, local copies, waits for them, and re-layouts: 16.4 us -> 2.42 us
where the time goes in v3:
time: 87.3 us; the launch traced here: 87.1 us
  Pallas kernels  83.4 us (96%)
  local copies, waits for them, and re-layouts  2.42 us (3%)
  between operations  1.29 us (1%)
    pallas_call x1, Pallas kernels, on_device(): pl.pallas_call(kernel, out_shape=(block, block), in_specs=[in_any] * 2 +...  83.4 us
    unnamed x4, local copies, waits for them, and re-layouts  2.42 us

profile of v3, /device:TPU:1, one launch (start us, length us, event | category | flops | bytes accessed | tf_op | source)
XLA Modules:
  0.0 87.1 jit_solution(17526131650649152164)
XLA Ops:
  1.3 83.4 %shard_map.185 = (f32[4,2,32,256]{3,2,1,0:T(8,128)}, f32[4,2,32,256]{3,2,1,0:T(8,128)}) custom-call(f32[4,2,32,256]{3,2,1,0:T(8,128)} %bitcast.3, f32[2,32,256]{2,1,0:T(8,128)} %init_hbm.1, s32[1]{0:T(128)S(6)} %copy.22.alpha_ref, f32[2,2,2,4]{3,2,1,0:T(2,128)} %mix_ref.1, f32[2,2,2,4]{3,2,1,0:T(2,128)} %back_ref.1, f32[2,2,2]{2,1,0:T(2,128)} %shifts_ref.1, ...), custom_call_target="tpu_custom_call" | custom-call | tf_op jit(solution)/shard_map/pallas_call | solution.py:441
  84.7 0.0 copy-start
  84.7 1.7 %copy.23 = f32[2,2,2,32,256]{4,3,2,1,0:T(8,128)} copy(f32[2,2,2,32,256]{4,3,2,1,0:T(8,128)} %bitcast.5) | data formatting | bytes 524288
  86.4 0.0 copy-done
  86.4 0.7 copy.24
Async XLA Ops:
  84.7 1.7 %copy-start = (f32[4,2,32,256]{3,2,1,0:T(8,128)S(1)}, f32[4,2,32,256]{3,2,1,0:T(8,128)}, u32[]{:S(2)}) copy-start(f32[4,2,32,256]{3,2,1,0:T(8,128)} %get-tuple-element.5) | copy-start | bytes 786436

commit v4 on v3

--- a/solution.py
+++ b/solution.py
@@ -2,6 +2,7 @@
 
 import jax
 import jax.numpy as jnp
+import ml_dtypes
 import numpy as np
 from jax import lax
 from jax.experimental import pallas as pl
@@ -17,7 +18,6 @@
 
 DIFFUSION = 0.5
 REACTION = 1.0
-HIGH = lax.Precision.HIGHEST
 
 
 def legendre_pair(degree, point):
@@ -91,7 +91,8 @@
 def tables():
     coll = np.array(collocation_matrix(NODES))
     sx, sy, sz = (sine_matrix(n) for n in (GX, GY, NZ))
-    kx = np.einsum("kx,fg->kfgx", sx, np.eye(8)).reshape(256, 256)
+    lam_z, lam_x, lam_y = (eigenvalues(n) for n in (NZ, GX, GY))
+    kx = np.einsum("pcx,fg->cpfgx", sx.reshape(16, 2, GX), np.eye(8)).reshape(2, 128, 256)
     n = np.arange(STEPS)
     real_dft = np.zeros((8, 2, STEPS))
     for q in range(8):
@@ -105,28 +106,47 @@
     last = np.zeros((NODES, 2, 2))
     last[:, 1, 1] = 1.0
     two = np.eye(2)
-    form = "qrsn,mtj,kl,zw->qkrmzstlnjw"
-    mu0 = -np.einsum(form, split, nodes, two, two).reshape(256, 256)
-    mu1 = np.einsum(form, shifted, last, two, two).reshape(256, 256)
-    mf = np.einsum(form, split, coll.reshape(NODES, 2, 2), two, two).reshape(256, 256)
-    mi = np.einsum("qrsn,mtj,kl,zw->stlnjwqkrmz", split, nodes, two, two).reshape(256, 256)
-    zf = np.einsum("rp,mn,ksz->rmkspnz", two, np.eye(4), sz.reshape(NZ, 32, 2)).reshape(512, 512)
-    lam_z, lam_x, lam_y = (eigenvalues(n) for n in (NZ, GX, GY))
-    lam_xy = np.repeat(lam_x, 8)[:, None] + lam_y[None]
+    form = "qrsn,mtj,zw->qrmzstnjw"
+    m0 = np.zeros((128, 2, 128))
+    m1 = np.zeros((128, 2, 128))
+    m0[:, 0] = -np.einsum(form, split, nodes, two).reshape(128, 128)
+    m0[:, 1] = np.einsum(form, split, coll.reshape(NODES, 2, 2), two).reshape(128, 128)
+    m1[:, 0] = np.einsum(form, shifted, last, two).reshape(128, 128)
+    m0, m1 = m0.reshape(128, 256), m1.reshape(128, 256)
+    mi = np.einsum("qrsn,mtj,zw->stnjwqrmz", split, nodes, two).reshape(128, 128)
+    zf = np.einsum("mn,ksz->mksnz", np.eye(4), sz.reshape(NZ, 32, 2)).reshape(256, 256)
+    lam_xy = lam_x.reshape(16, 2).T[:, :, None, None] + lam_y
+    lam_xy = np.broadcast_to(lam_xy, (2, 16, 8, 256)).reshape(2, 128, 256)
     lam_zy = lam_z[None, :, None] + lam_y.reshape(2, 1, 128)
     lam_x = np.broadcast_to(lam_x[:, None, None], (GX, 8, 128))
     start = np.linalg.solve(coll, np.ones(NODES))
-    arrays = dict(sy=sy, kx=kx, lam_xy=lam_xy, mu0=mu0, mu1=mu1, mf=mf, zf=zf, zt=zf.T, mi=mi,
-                  kt=kx.T, lam_zy=lam_zy, lam_x=lam_x)
-    return coll, start, {k: np.asarray(v, np.float32) for k, v in arrays.items()}
+    exact = dict(lam_xy=lam_xy, m0=m0, m1=m1, mi=mi, lam_zy=lam_zy, lam_x=lam_x)
+    arrays = dict(sy=halves(sy), kx=halves(kx))
+    arrays.update({k: np.asarray(v, np.float32) for k, v in exact.items()})
+    kt = kx.transpose(0, 2, 1)
+    arrays.update(zf=halves(zf), zt=halves(zf.T), kt=halves(kt))
+    return coll, start, arrays
+
+
+def halves(matrix):
+    matrix = np.asarray(matrix, np.float32)
+    upper = matrix.astype(ml_dtypes.bfloat16)
+    lower = (matrix - upper.astype(np.float32)).astype(ml_dtypes.bfloat16)
+    return np.stack([upper, lower])
 
 
 COLL, START, TABLES = tables()
 NAMES = tuple(TABLES)
 
 
-def dot(a, b):
-    return jnp.dot(a, b, precision=HIGH, preferred_element_type=jnp.float32)
+def parts(x):
+    upper = x.astype(jnp.bfloat16)
+    return upper, (x - upper.astype(jnp.float32)).astype(jnp.bfloat16)
+
+
+def dot3(a, b):
+    one = lambda x, y: jnp.dot(x, y, preferred_element_type=jnp.float32)
+    return one(a[0], b[0]) + (one(a[0], b[1]) + one(a[1], b[0]))
 
 
 def horner_tables(q, params, coef, tab, lam):
@@ -198,10 +218,11 @@
     refs = refs[2:]
     held = dict(zip(NAMES, refs[: len(NAMES)]))
     refs = refs[len(NAMES) :]
-    (u_ref, init_ref, su, ru, sf, rf, sp, rp, s2, r2, s3, r3, s4, r4, halo, grid, ub, wb, whalo, before, coef, tab,
-     sw, ow, load_sem, send_sem, recv_sem) = refs
+    (u_ref, init_ref, su, sf, r1, sp, rp, s2, r2, s3, r3, s4, r4, halo, grid, ub, wb, whalo, before, coef, tab,
+     mm, mb, sw, ow, load_sem, send_sem, recv_sem) = refs
     step, node, space = (lax.axis_index(a) for a in ("step", "node", "space"))
     me = step * 2 + node
+    q, chunk, half = space // 4, (space // 2) % 2, space % 2
 
     load_u = pltpu.make_async_copy(u_hbm, u_ref, load_sem.at[len(NAMES)])
     load_init = pltpu.make_async_copy(init_hbm, init_ref, load_sem.at[len(NAMES) + 1])
@@ -232,15 +253,31 @@
 
     lax.fori_loop(1, 16, greet_group, 0)
     lax.fori_loop(1, 32, greet_space, 0)
+
+    load_u.wait()
+    get("sy"), get("kx")
+    sy = (held["sy"][0], held["sy"][1])
+
+    def to_sines(field):
+        return parts(dot3(parts(field), sy))
+
+    def x_sines(c, rows):
+        return dot3((held["kx"][0, c], held["kx"][1, c]), rows)
+
+    rows = to_sines(u_ref[...].reshape(256, 256))
+    for c in range(2):
+        su[c] = x_sines(c, rows).reshape(16, 8, 256)
     pl.semaphore_wait(barrier, 46)
 
-    def remote(src, dst, sem, device):
+    def remote(src, dst, sem, device, recv=None):
+        recv = sem if recv is None else recv
         return pltpu.make_async_remote_copy(
-            src_ref=src, dst_ref=dst, send_sem=send_sem.at[sem], recv_sem=recv_sem.at[sem], device_id=device
+            src_ref=src, dst_ref=dst, send_sem=send_sem.at[sem], recv_sem=recv_sem.at[recv], device_id=device
         )
 
     up, down = {"space": (space + 1) % 32}, {"space": (space + 31) % 32}
-    HALO_UP, HALO_DOWN, GROUP_U, GROUP_F, PARAMS, SPACE, BACK, CORR, OTHER, W_UP, W_DOWN, BEFORE = range(12)
+    HALO_UP, HALO_DOWN, OTHER, PARAMS, SPACE, W_UP, W_DOWN, BEFORE = range(8)
+    FIELD, FORCE, BACK, CORR = 8, 10, 12, 14
     pending = [
         remote(u_hbm.at[:, 1], halo.at[0], HALO_UP, up),
         remote(u_hbm.at[:, 0], halo.at[1], HALO_DOWN, down),
@@ -253,30 +290,38 @@
             other, device = group_id(d)
             remote(src.at[other], dst.at[me], sem, device).start()
             return 0
+
         lax.fori_loop(1, 16, body, 0)
         dst[me] = src[me]
 
-    def to_space(src, dst, sem):
-        def body(d, _):
-            other = (space + d) % 32
-            remote(src.at[other], dst.at[space], sem, {"space": other}).start()
-            return 0
-        lax.fori_loop(1, 32, body, 0)
-        dst[space] = src[space]
+    def block_of(ref, count):
+        return ref.at[pl.ds(0, count)]
 
     def arrived(ref, sem, count):
-        part = ref.at[pl.ds(0, count)]
+        part = block_of(ref, count)
         remote(part, part, sem, up).wait_recv()
 
     def sent(ref, sem, count):
-        part = ref.at[pl.ds(0, count)]
+        part = block_of(ref, count)
         remote(part, part, sem, up).wait_send()
 
-    load_u.wait()
-    sy, kx = get("sy"), get("kx")
-    uh = dot(kx[...], dot(u_ref[...].reshape(256, 256), sy[...]))
-    su[...] = uh.reshape(16, 16, 256)
-    to_group(su, ru, GROUP_U)
+    for c in range(2):
+        to_group(su.at[c], r1.at[c, 0], FIELD + c)
+
+    pack_params(node, mix_ref, back_ref, shifts_ref, sp)
+
+    def send_params(d, _):
+        remote(sp, rp.at[me], PARAMS, group_id(d)[1]).start()
+        return 0
+
+    rate = alpha_ref[0].astype(jnp.float32) * (math.log(2.0) / 16.0 / STEPS)
+    col = lax.broadcasted_iota(jnp.int32, (1, 256), 1) % 128
+    when = (2 * (col // 16) + (col // 4) % 2).astype(jnp.float32)
+    scaled = get("m0")[...] * jnp.exp(-rate * when) + get("m1")[...] * jnp.exp(-rate * (when + 1.0))
+    mm[0], mm[1] = parts(scaled)
+    row = lax.broadcasted_iota(jnp.int32, (128, 128), 0)
+    when = (2 * (row // 16) + (row // 4) % 2).astype(jnp.float32)
+    mb[0], mb[1] = parts(get("mi")[...] * (jnp.exp(rate * when) * (1.0 / STEPS)))
 
     low = jnp.where(space == 0, 0.0, DIFFUSION)
     high = jnp.where(space == 31, 0.0, DIFFUSION)
@@ -284,6 +329,7 @@
         jnp.where(step == 0, jnp.where(node == 0, START[m], START[2 + m]), 0.0).astype(jnp.float32) for m in range(2)
     ]
     load_init.wait()
+    get("lam_xy")
     pending[0].wait_recv()
     pending[1].wait_recv()
     for nm in range(4):
@@ -294,86 +340,95 @@
             if nm < 2:
                 value = value + begin[nm] * init_ref[z]
             grid[nm * 2 + z] = value
-    fh = dot(kx[...], dot(grid[...].reshape(256, 256), sy[...]))
-    fh = fh + DIFFUSION * get("lam_xy")[...] * su[...].reshape(256, 256)
-    sf[...] = fh.reshape(16, 16, 256)
-    to_group(sf, rf, GROUP_F)
-
-    pack_params(node, mix_ref, back_ref, shifts_ref, sp)
-
-    def send_params(d, _):
-        remote(sp, rp.at[me], PARAMS, group_id(d)[1]).start()
-        return 0
-
+    rows = to_sines(grid[...].reshape(256, 256))
+    for c in range(2):
+        value = x_sines(c, rows) + DIFFUSION * held["lam_xy"][c] * su[c].reshape(128, 256)
+        sf[c] = value.reshape(16, 8, 256)
+        to_group(sf.at[c], r1.at[c, 1], FORCE + c)
     lax.fori_loop(1, 16, send_params, 0)
     rp[me] = sp[...]
 
-    rate = alpha_ref[0].astype(jnp.float32) * (math.log(2.0) / 16.0 / STEPS)
-    col = lax.broadcasted_iota(jnp.int32, (1, 256), 1)
-    when = (2 * (col // 32) + (col // 4) % 2).astype(jnp.float32)
-    scale0, scale1 = jnp.exp(-rate * when), jnp.exp(-rate * (when + 1.0))
-    mu = get("mu0")[...] * scale0 + get("mu1")[...] * scale1
-    mf = get("mf")[...] * scale0
-    arrived(ru, GROUP_U, 15)
-    spec = dot(mu, ru[...].reshape(256, 256))
-    arrived(rf, GROUP_F, 15)
-    spec = spec + dot(mf, rf[...].reshape(256, 256))
-    for h in range(2):
-        s2[:, h] = spec[:, h * 128 : h * 128 + 128].reshape(16, 16, 128)
-    s2_flat, r2_flat = s2.reshape(32, 16, 128), r2
-    to_space(s2_flat, r2_flat, SPACE)
+    for c in range(2):
+        arrived(r1.at[c, 0], FIELD + c, 15)
+        arrived(r1.at[c, 1], FORCE + c, 15)
+        spec = dot3((mm[0], mm[1]), parts(r1[c].reshape(256, 256))).reshape(8, 2, 8, 256)
+        for h in range(2):
+            for part in range(2):
+                s2[c, h, :, :, part * 128 : part * 128 + 128] = spec[:, part, :, h * 128 : h * 128 + 128]
+        for h in range(2):
+            def send_spec(d, _):
+                other = (q + d) % 8
+                place = 4 * other + 2 * c + h
+                @pl.when(place != space)
+                def _():
+                    remote(s2.at[c, h, other], r2.at[space], SPACE, {"space": place}).start()
+                return 0
+
+            lax.fori_loop(0, 8, send_spec, 0)
+    r2[space] = s2[chunk, half, q]
     other_u = remote(u_hbm, ub.at[node], OTHER, {"node": 1 - node})
     other_u.start()
     ub[node] = u_ref[...]
 
     arrived(rp, PARAMS, 15)
-    q = space // 4
-    lam = get("lam_zy")[space % 2] + jnp.broadcast_to(
-        get("lam_x")[2 * me + (space // 2) % 2][0:1], (64, 128))
+    lam = get("lam_zy")[half] + jnp.broadcast_to(get("lam_x")[2 * me + chunk][0:1], (64, 128))
     horner_tables(q, rp, coef, tab, lam)
-    row = lax.broadcasted_iota(jnp.int32, (256, 256), 0)
-    when = (2 * (row // 32) + (row // 4) % 2).astype(jnp.float32)
-    held["mi"][...] = get("mi")[...] * (jnp.exp(rate * when) * (1.0 / STEPS))
-
-    zf, zt = get("zf"), get("zt")
-    arrived(r2_flat, SPACE, 31)
-    sw[...] = dot(zf[...], r2[...].reshape(512, 128)).reshape(8, 64, 128)
+    get("zf"), get("zt")
+    arrived(r2, SPACE, 31)
+    sw[...] = dot3((held["zf"][0], held["zf"][1]), parts(r2[...].reshape(256, 256))).reshape(4, 64, 256)
 
     def solve(z, _):
         at = pl.ds(pl.multiple_of(z * 8, 8), 8)
-        s = [sw[i, at, :] for i in range(8)]
+        re_in = [sw[i, at, 0:128] for i in range(4)]
+        im_in = [sw[i, at, 128:256] for i in range(4)]
         for i in range(4):
             re = im = None
             for j in range(4):
                 a, e, d = (tab[c, 4 * i + j, at, :] for c in range(3))
-                tre, tim = a * s[j] - e * s[4 + j], e * s[j] + d * s[4 + j]
+                tre, tim = a * re_in[j] - e * im_in[j], e * re_in[j] + d * im_in[j]
                 re, im = (tre, tim) if re is None else (re + tre, im + tim)
-            ow[i, at, :] = re
-            ow[4 + i, at, :] = im
+            ow[i, at, 0:128] = re
+            ow[i, at, 128:256] = im
         return 0
 
     lax.fori_loop(0, 8, solve, 0)
-    s3[...] = dot(zt[...], ow[...].reshape(512, 128)).reshape(32, 16, 128)
-    to_space(s3, r3, BACK)
-    kt = get("kt")
-    arrived(r3, BACK, 31)
-    for h in range(2):
-        part = r3[...].reshape(16, 2, 16, 128)[:, h].reshape(256, 128)
-        s4[:, :, :, h * 128 : h * 128 + 128] = dot(held["mi"][...], part).reshape(8, 2, 16, 128)
-
-    def send_corr(d, _):
-        other, device = group_id(d)
-        remote(s4.at[other // 2], r4.at[:, me], CORR, device).start()
+    value = dot3((held["zt"][0], held["zt"][1]), parts(ow[...].reshape(256, 256))).reshape(32, 8, 256)
+    for part in range(2):
+        s3[:, part] = value[:, :, part * 128 : part * 128 + 128]
+
+    def send_back(d, _):
+        other = (space + d) % 32
+        remote(s3.at[other], r3.at[chunk, half, q], BACK, {"space": other}, BACK + chunk).start()
         return 0
 
-    lax.fori_loop(1, 16, send_corr, 0)
-    r4[:, me] = s4[step]
+    lax.fori_loop(1, 32, send_back, 0)
+    r3[chunk, half, q] = s3[space]
+    get("kt")
+    for c in range(2):
+        for here in range(2):
+            @pl.when((chunk == c) if here else (chunk != c))
+            def _():
+                part = block_of(s3, 16 - here)
+                remote(part, part, BACK, up, BACK + c).wait_recv()
+        for h in range(2):
+            value = dot3((mb[0], mb[1]), parts(r3[c, h].reshape(128, 128)))
+            s4[c, :, :, :, h * 128 : h * 128 + 128] = value.reshape(8, 2, 8, 128)
+
+        def send_corr(d, _):
+            other, device = group_id(d)
+            remote(s4.at[c, other // 2], r4.at[c, :, me], CORR + c, device).start()
+            return 0
+
+        lax.fori_loop(1, 16, send_corr, 0)
+        r4[c, :, me] = s4[c, step]
     other_u.wait_recv()
-    whole = r4.at[:, pl.ds(0, 15)]
-    remote(whole, whole, CORR, up).wait_recv()
-    for g in range(2):
-        d = dot(dot(kt[...], r4[g].reshape(256, 256)), sy[...])
-        ub[g] = ub[g] + d.reshape(4, 2, 32, 256)
+    for c in range(2):
+        whole = r4.at[c, :, pl.ds(0, 15)]
+        remote(whole, whole, CORR + c, up).wait_recv()
+        for g in range(2):
+            rows = to_sines(r4[c, g].reshape(128, 256))
+            d = dot3((held["kt"][0, c], held["kt"][1, c]), rows)
+            ub[g] = ub[g] + d.reshape(4, 2, 32, 256)
     out_u[...] = ub[node]
 
     weight = [
@@ -424,12 +479,14 @@
 
     for copy in pending + last + [other_u]:
         copy.wait_send()
-    sent(su, GROUP_U, 15)
-    sent(sf, GROUP_F, 15)
+    for c in range(2):
+        sent(su.at[c], FIELD + c, 15)
+        sent(sf.at[c], FORCE + c, 15)
+        whole = r4.at[c, :, pl.ds(0, 15)]
+        remote(whole, whole, CORR + c, up).wait_send()
     sent(rp, PARAMS, 15)
-    sent(s3, SPACE, 31)
+    sent(r2, SPACE, 31)
     sent(s3, BACK, 31)
-    remote(whole, whole, CORR, up).wait_send()
 
 
 def on_device(iterate, initial_value, alpha_power, node_mix, node_back, shifts):
@@ -443,18 +500,20 @@
         out_shape=(block, block),
         in_specs=[in_any] * 2 + [in_smem] * 4 + [in_any] * len(NAMES),
         out_specs=(in_vmem, in_vmem),
-        scratch_shapes=[vmem(*TABLES[name].shape) for name in NAMES]
+        scratch_shapes=[pltpu.VMEM(TABLES[name].shape, TABLES[name].dtype) for name in NAMES]
         + [vmem(4, 2, 32, 256), vmem(2, 32, 256)]
-        + [vmem(16, 16, 256)] * 4
+        + [vmem(2, 16, 8, 256)] * 2
+        + [vmem(2, 2, 16, 8, 256)]
         + [vmem(8, 128), vmem(16, 8, 128)]
-        + [vmem(16, 2, 16, 128), vmem(32, 16, 128)]
-        + [vmem(32, 16, 128)] * 2
-        + [vmem(8, 2, 16, 256), vmem(2, 16, 16, 256)]
+        + [vmem(2, 2, 8, 8, 256), vmem(32, 8, 256)]
+        + [vmem(32, 2, 8, 128), vmem(2, 2, 8, 2, 8, 128)]
+        + [vmem(2, 8, 2, 8, 256), vmem(2, 2, 16, 8, 256)]
         + [vmem(2, 4, 32, 256), vmem(8, 32, 256)]
         + [vmem(2, 4, 2, 32, 256), vmem(4, 2, 32, 256), vmem(2, 4, 32, 256), vmem(2, 32, 256)]
         + [vmem(3, 8, 128), vmem(3, 16, 64, 128)]
-        + [vmem(8, 64, 128)] * 2
-        + [pltpu.SemaphoreType.DMA((len(NAMES) + 2,)), pltpu.SemaphoreType.DMA((12,)), pltpu.SemaphoreType.DMA((12,))],
+        + [pltpu.VMEM((2, 128, 256), jnp.bfloat16), pltpu.VMEM((2, 128, 128), jnp.bfloat16)]
+        + [vmem(4, 64, 256)] * 2
+        + [pltpu.SemaphoreType.DMA((len(NAMES) + 2,)), pltpu.SemaphoreType.DMA((16,)), pltpu.SemaphoreType.DMA((16,))],
         compiler_params=pltpu.CompilerParams(
             collective_id=0, has_side_effects=True, vmem_limit_bytes=63 * 1024 * 1024
         ),

time: 87.3 us -> 80.1 us (0.918)
  Pallas kernels: 83.4 us -> 76.2 us
    pallas_call x1, Pallas kernels: 83.4 us -> 76.2 us  [on_device(): pl.pallas_call(kernel, out_shape=(block, block), in_specs=[in_any] * 2 +...]
where the time goes in v4:
time: 80.1 us; the launch traced here: 79.9 us
  Pallas kernels  76.2 us (95%)
  local copies, waits for them, and re-layouts  2.42 us (3%)
  between operations  1.29 us (2%)
    pallas_call x1, Pallas kernels, on_device(): pl.pallas_call(kernel, out_shape=(block, block), in_specs=[in_any] * 2 +...  76.2 us
    unnamed x4, local copies, waits for them, and re-layouts  2.42 us

profile of v4, /device:TPU:1, one launch (start us, length us, event | category | flops | bytes accessed | tf_op | source)
XLA Modules:
  0.0 79.9 jit_solution(9870137360444150708)
XLA Ops:
  1.3 76.2 %shard_map.176 = (f32[4,2,32,256]{3,2,1,0:T(8,128)}, f32[4,2,32,256]{3,2,1,0:T(8,128)}) custom-call(f32[4,2,32,256]{3,2,1,0:T(8,128)} %bitcast.3, f32[2,32,256]{2,1,0:T(8,128)} %init_hbm.1, s32[1]{0:T(128)S(6)} %copy.21.alpha_ref, f32[2,2,2,4]{3,2,1,0:T(2,128)} %mix_ref.1, f32[2,2,2,4]{3,2,1,0:T(2,128)} %back_ref.1, f32[2,2,2]{2,1,0:T(2,128)} %shifts_ref.1, ...), custom_call_target="tpu_custom_call" | custom-call | tf_op jit(solution)/shard_map/pallas_call | solution.py:498
  77.5 0.0 copy-start
  77.5 1.7 %copy.22 = f32[2,2,2,32,256]{4,3,2,1,0:T(8,128)} copy(f32[2,2,2,32,256]{4,3,2,1,0:T(8,128)} %bitcast.5) | data formatting | bytes 524288
  79.2 0.0 copy-done
  79.2 0.7 copy.23
Async XLA Ops:
  77.5 1.7 %copy-start = (f32[4,2,32,256]{3,2,1,0:T(8,128)S(1)}, f32[4,2,32,256]{3,2,1,0:T(8,128)}, u32[]{:S(2)}) copy-start(f32[4,2,32,256]{3,2,1,0:T(8,128)} %get-tuple-element.5) | copy-start | bytes 786436

commit v5 on v4

--- a/solution.py
+++ b/solution.py
@@ -211,15 +211,15 @@
     out[...] = acc
 
 
-def kernel(u_hbm, init_hbm, alpha_ref, mix_ref, back_ref, shifts_ref, *refs):
+def kernel(u_hbm, init_hbm, alpha_hbm, mix_hbm, back_hbm, shifts_hbm, *refs):
     consts = dict(zip(NAMES, refs[: len(NAMES)]))
     refs = refs[len(NAMES) :]
     out_u, out_r = refs[:2]
     refs = refs[2:]
     held = dict(zip(NAMES, refs[: len(NAMES)]))
     refs = refs[len(NAMES) :]
-    (u_ref, init_ref, su, sf, r1, sp, rp, s2, r2, s3, r3, s4, r4, halo, grid, ub, wb, whalo, before, coef, tab,
-     mm, mb, sw, ow, load_sem, send_sem, recv_sem) = refs
+    (u_ref, init_ref, su, sf, r1, sp, rp, s2, r2, s3, r3, s4, r4, halo, grid, ub, wb, wedge, whalo, before, coef, tab,
+     mm, mb, sw, ow, alpha_ref, mix_ref, back_ref, shifts_ref, heard, load_sem, send_sem, recv_sem) = refs
     step, node, space = (lax.axis_index(a) for a in ("step", "node", "space"))
     me = step * 2 + node
     q, chunk, half = space // 4, (space // 2) % 2, space % 2
@@ -230,9 +230,13 @@
     loads = {}
     for index, name in enumerate(NAMES):
         loads[name] = pltpu.make_async_copy(consts[name], held[name], load_sem.at[index])
-        loads[name].start()
-    load_init.start()
-
+    loads["sy"].start()
+    loads["kx"].start()
+    small = [
+        pltpu.make_async_copy(src, dst, load_sem.at[len(NAMES) + 2 + i])
+        for i, (src, dst) in enumerate(
+            [(alpha_hbm, alpha_ref), (mix_hbm, mix_ref), (back_hbm, back_ref), (shifts_hbm, shifts_ref)])
+    ]
     def get(name):
         loads[name].wait()
         return held[name]
@@ -247,12 +251,19 @@
         pl.semaphore_signal(barrier, inc=1, device_id=group_id(d)[1])
         return 0
 
-    def greet_space(d, _):
-        pl.semaphore_signal(barrier, inc=1, device_id={"space": (space + d) % 32})
-        return 0
+    def near(d):
+        return {"space": (space + d) % 32}
 
     lax.fori_loop(1, 16, greet_group, 0)
-    lax.fori_loop(1, 32, greet_space, 0)
+    for d in (1, 31):
+        pl.semaphore_signal(barrier, inc=1, device_id=near(d))
+
+    def tell(turn):
+        for d in (1 << turn, 32 - (1 << turn)):
+            pl.semaphore_signal(heard.at[turn], inc=1, device_id=near(d))
+
+    def hear(turn):
+        pl.semaphore_wait(heard.at[turn], 2)
 
     load_u.wait()
     get("sy"), get("kx")
@@ -267,7 +278,13 @@
     rows = to_sines(u_ref[...].reshape(256, 256))
     for c in range(2):
         su[c] = x_sines(c, rows).reshape(16, 8, 256)
-    pl.semaphore_wait(barrier, 46)
+    load_init.start()
+    for copy in small:
+        copy.start()
+    for name in NAMES[2:]:
+        loads[name].start()
+    pl.semaphore_wait(barrier, 17)
+    tell(0)
 
     def remote(src, dst, sem, device, recv=None):
         recv = sem if recv is None else recv
@@ -276,14 +293,29 @@
         )
 
     up, down = {"space": (space + 1) % 32}, {"space": (space + 31) % 32}
-    HALO_UP, HALO_DOWN, OTHER, PARAMS, SPACE, W_UP, W_DOWN, BEFORE = range(8)
-    FIELD, FORCE, BACK, CORR = 8, 10, 12, 14
+    HALO_UP, HALO_DOWN, PARAMS, SPACE, W_UP, W_DOWN, BEFORE = range(7)
+    OTHER, FIELD, FORCE, BACK, CORR = 8, 10, 12, 14, 16
     pending = [
         remote(u_hbm.at[:, 1], halo.at[0], HALO_UP, up),
         remote(u_hbm.at[:, 0], halo.at[1], HALO_DOWN, down),
     ]
-    for copy in pending:
-        copy.start()
+    not_first, not_last = space > 0, space < 31
+
+    @pl.when(not_last)
+    def _():
+        pending[0].start()
+
+    @pl.when(not_first)
+    def _():
+        pending[1].start()
+
+    @pl.when(space == 0)
+    def _():
+        halo[0] = jnp.zeros((4, 32, 256), jnp.float32)
+
+    @pl.when(space == 31)
+    def _():
+        halo[1] = jnp.zeros((4, 32, 256), jnp.float32)
 
     def to_group(src, dst, sem):
         def body(d, _):
@@ -307,7 +339,11 @@
 
     for c in range(2):
         to_group(su.at[c], r1.at[c, 0], FIELD + c)
-
+    hear(0)
+    tell(1)
+
+    for copy in small:
+        copy.wait()
     pack_params(node, mix_ref, back_ref, shifts_ref, sp)
 
     def send_params(d, _):
@@ -323,19 +359,26 @@
     when = (2 * (row // 16) + (row // 4) % 2).astype(jnp.float32)
     mb[0], mb[1] = parts(get("mi")[...] * (jnp.exp(rate * when) * (1.0 / STEPS)))
 
-    low = jnp.where(space == 0, 0.0, DIFFUSION)
-    high = jnp.where(space == 31, 0.0, DIFFUSION)
     begin = [
         jnp.where(step == 0, jnp.where(node == 0, START[m], START[2 + m]), 0.0).astype(jnp.float32) for m in range(2)
     ]
     load_init.wait()
     get("lam_xy")
-    pending[0].wait_recv()
-    pending[1].wait_recv()
+    hear(1)
+    tell(2)
+
+    @pl.when(not_first)
+    def _():
+        pending[0].wait_recv()
+
+    @pl.when(not_last)
+    def _():
+        pending[1].wait_recv()
+
     for nm in range(4):
         for z in range(2):
             u = u_ref[nm, z]
-            beside = DIFFUSION * u_ref[nm, 1 - z] + (low if z == 0 else high) * halo[z, nm]
+            beside = DIFFUSION * u_ref[nm, 1 - z] + DIFFUSION * halo[z, nm]
             value = beside - (6.0 * DIFFUSION - REACTION) * u - REACTION * (u * u * u)
             if nm < 2:
                 value = value + begin[nm] * init_ref[z]
@@ -345,6 +388,9 @@
         value = x_sines(c, rows) + DIFFUSION * held["lam_xy"][c] * su[c].reshape(128, 256)
         sf[c] = value.reshape(16, 8, 256)
         to_group(sf.at[c], r1.at[c, 1], FORCE + c)
+        if c == 0:
+            hear(2)
+            tell(3)
     lax.fori_loop(1, 16, send_params, 0)
     rp[me] = sp[...]
 
@@ -355,6 +401,8 @@
         for h in range(2):
             for part in range(2):
                 s2[c, h, :, :, part * 128 : part * 128 + 128] = spec[:, part, :, h * 128 : h * 128 + 128]
+        if c == 0:
+            hear(3)
         for h in range(2):
             def send_spec(d, _):
                 other = (q + d) % 8
@@ -366,8 +414,10 @@
 
             lax.fori_loop(0, 8, send_spec, 0)
     r2[space] = s2[chunk, half, q]
-    other_u = remote(u_hbm, ub.at[node], OTHER, {"node": 1 - node})
-    other_u.start()
+    other_u = [
+        remote(u_hbm.at[pl.ds(2 * i, 2)], ub.at[node, pl.ds(2 * i, 2)], OTHER + i, {"node": 1 - node}) for i in range(2)
+    ]
+    other_u[0].start()
     ub[node] = u_ref[...]
 
     arrived(rp, PARAMS, 15)
@@ -402,6 +452,7 @@
         return 0
 
     lax.fori_loop(1, 32, send_back, 0)
+    other_u[1].start()
     r3[chunk, half, q] = s3[space]
     get("kt")
     for c in range(2):
@@ -421,7 +472,8 @@
 
         lax.fori_loop(1, 16, send_corr, 0)
         r4[c, :, me] = s4[c, step]
-    other_u.wait_recv()
+    for copy in other_u:
+        copy.wait_recv()
     for c in range(2):
         whole = r4.at[c, :, pl.ds(0, 15)]
         remote(whole, whole, CORR + c, up).wait_recv()
@@ -429,7 +481,7 @@
             rows = to_sines(r4[c, g].reshape(128, 256))
             d = dot3((held["kt"][0, c], held["kt"][1, c]), rows)
             ub[g] = ub[g] + d.reshape(4, 2, 32, 256)
-    out_u[...] = ub[node]
+    out_u[...] = ub[node] - u_ref[...]
 
     weight = [
         [jnp.where(node == 0, COLL[m][j], COLL[2 + m][j]).astype(jnp.float32) for j in range(4)] for m in range(2)
@@ -438,14 +490,20 @@
     def nodes_at(n, z):
         return [ub[j // 2, 2 * n + j % 2, z] for j in range(4)]
 
+    seam_up, seam_down = (space % 16) // 15, (space + 15) % 16 // 15
+    above = {"space": (space + 1) % 32, "node": (node + seam_up) % 2}
+    below = {"space": (space + 31) % 32, "node": (node + seam_down) % 2}
+    target = [(node + seam_down) % 2, (node + seam_up) % 2]
     for n in range(2):
         for z in range(2):
             u = nodes_at(n, z)
             for m in range(2):
                 wb[2 * n + m, z] = sum(weight[m][j] * u[j] for j in range(4))
+                rows = [jnp.where(target[z] == 0, COLL[m][j], COLL[2 + m][j]).astype(jnp.float32) for j in range(4)]
+                wedge[z, 2 * n + m] = sum(rows[j] * u[j] for j in range(4))
     last = [
-        remote(wb.at[:, 1], whalo.at[0], W_UP, up),
-        remote(wb.at[:, 0], whalo.at[1], W_DOWN, down),
+        remote(wedge.at[1], whalo.at[0], W_UP, above),
+        remote(wedge.at[0], whalo.at[1], W_DOWN, below),
         remote(ub.at[1, 3], before, BEFORE, {"step": (step + 1) % 8}),
     ]
     for copy in last:
@@ -465,19 +523,29 @@
                     + jnp.where(y == 255, 0.0, pltpu.roll(w, 255, 1))
                 )
                 value = DIFFUSION * beside - (6.0 * DIFFUSION - REACTION) * w
-                value = value - REACTION * sum(weight[m][j] * cubes[j] for j in range(4)) - ub[node, 2 * n + m, z]
+                value = value - REACTION * sum(weight[m][j] * cubes[j] for j in range(4))
                 if n == 1:
                     value = value + ub[1, 1, z]
                 out_r[2 * n + m, z] = value
     for copy in last:
         copy.wait_recv()
+    low = jnp.where(space == 0, 0.0, DIFFUSION)
+    high = jnp.where(space == 31, 0.0, DIFFUSION)
     for z in range(2):
         opening = jnp.where(step == 0, init_ref[z], before[z])
         for nm in range(4):
             edge = (low if z == 0 else high) * whalo[z, nm]
             out_r[nm, z] = out_r[nm, z] + (edge + opening if nm < 2 else edge)
 
-    for copy in pending + last + [other_u]:
+    @pl.when(not_last)
+    def _():
+        pending[0].wait_send()
+
+    @pl.when(not_first)
+    def _():
+        pending[1].wait_send()
+
+    for copy in last + other_u:
         copy.wait_send()
     for c in range(2):
         sent(su.at[c], FIELD + c, 15)
@@ -494,11 +562,11 @@
     f32 = jnp.float32
     vmem = lambda *shape: pltpu.VMEM(shape, f32)
     block = jax.ShapeDtypeStruct((4, 2, 32, 256), f32)
-    in_vmem, in_smem, in_any = (pl.BlockSpec(memory_space=m) for m in (pltpu.VMEM, pltpu.SMEM, pl.ANY))
-    updated, residual = pl.pallas_call(
+    in_vmem, in_any = (pl.BlockSpec(memory_space=m) for m in (pltpu.VMEM, pltpu.HBM))
+    correction, rest = pl.pallas_call(
         kernel,
         out_shape=(block, block),
-        in_specs=[in_any] * 2 + [in_smem] * 4 + [in_any] * len(NAMES),
+        in_specs=[in_any] * (6 + len(NAMES)),
         out_specs=(in_vmem, in_vmem),
         scratch_shapes=[pltpu.VMEM(TABLES[name].shape, TABLES[name].dtype) for name in NAMES]
         + [vmem(4, 2, 32, 256), vmem(2, 32, 256)]
@@ -509,16 +577,20 @@
         + [vmem(32, 2, 8, 128), vmem(2, 2, 8, 2, 8, 128)]
         + [vmem(2, 8, 2, 8, 256), vmem(2, 2, 16, 8, 256)]
         + [vmem(2, 4, 32, 256), vmem(8, 32, 256)]
-        + [vmem(2, 4, 2, 32, 256), vmem(4, 2, 32, 256), vmem(2, 4, 32, 256), vmem(2, 32, 256)]
+        + [vmem(2, 4, 2, 32, 256), vmem(4, 2, 32, 256)]
+        + [vmem(2, 4, 32, 256)] * 2 + [vmem(2, 32, 256)]
         + [vmem(3, 8, 128), vmem(3, 16, 64, 128)]
         + [pltpu.VMEM((2, 128, 256), jnp.bfloat16), pltpu.VMEM((2, 128, 128), jnp.bfloat16)]
         + [vmem(4, 64, 256)] * 2
-        + [pltpu.SemaphoreType.DMA((len(NAMES) + 2,)), pltpu.SemaphoreType.DMA((16,)), pltpu.SemaphoreType.DMA((16,))],
+        + [pltpu.SMEM((1,), jnp.int32), pltpu.SMEM((2, 2, 2, 4), f32), pltpu.SMEM((2, 2, 2, 4), f32), pltpu.SMEM((2, 2, 2), f32)]
+        + [pltpu.SemaphoreType.REGULAR((4,))]
+        + [pltpu.SemaphoreType.DMA((len(NAMES) + 6,)), pltpu.SemaphoreType.DMA((18,)), pltpu.SemaphoreType.DMA((18,))],
         compiler_params=pltpu.CompilerParams(
             collective_id=0, has_side_effects=True, vmem_limit_bytes=63 * 1024 * 1024
         ),
     )(iterate.reshape(4, 2, 32, 256), initial_value, alpha_power, node_mix, node_back, shifts, *consts)
-    return updated.reshape(iterate.shape), residual.reshape(iterate.shape)
+    updated = iterate + correction.reshape(iterate.shape)
+    return updated, rest.reshape(iterate.shape) - updated
 
 
 def solution(mesh):

time: 80.1 us -> 75.9 us (0.948)
  Pallas kernels: 76.2 us -> 72.5 us
  local copies, waits for them, and re-layouts: 2.42 us -> 0.01 us
  other arithmetic: 0 us -> 1.88 us
    pallas_call x1, Pallas kernels: 76.2 us -> 72.5 us  [on_device(): pl.pallas_call(kernel, out_shape=(block, block), in_specs=[in_any] * (6 +...]
    unnamed x4 -> x2, local copies, waits for them, and re-layouts: 2.42 us -> 0.01 us
    sub x0 -> x1, other arithmetic: none -> 1.88 us  [on_device(): return (updated, rest.reshape(iterate.shape) - updated)]
where the time goes in v5:
time: 75.9 us; the launch traced here: 75.7 us
  Pallas kernels  72.5 us (96%)
  other arithmetic  1.88 us (2%)
  between operations  1.3 us (2%)
    pallas_call x1, Pallas kernels, on_device(): pl.pallas_call(kernel, out_shape=(block, block), in_specs=[in_any] * (6 +...  72.5 us
    sub x1, other arithmetic, on_device(): return (updated, rest.reshape(iterate.shape) - updated)  1.88 us

profile of v5, /device:TPU:1, one launch (start us, length us, event | category | flops | bytes accessed | tf_op | source)
XLA Modules:
  0.0 75.7 jit_solution(10593719158595358728)
XLA Ops:
  1.3 0.0 copy-start
  1.3 72.5 %shard_map.176 = (f32[4,2,32,256]{3,2,1,0:T(8,128)}, f32[4,2,32,256]{3,2,1,0:T(8,128)}) custom-call(f32[4,2,32,256]{3,2,1,0:T(8,128)} %bitcast.3, f32[2,32,256]{2,1,0:T(8,128)} %init_hbm.1, s32[1]{0:T(128)S(6)} %copy.19.alpha_hbm, f32[2,2,2,4]{3,2,1,0:T(2,128)} %mix_hbm.1, f32[2,2,2,4]{3,2,1,0:T(2,128)} %back_hbm.1, f32[2,2,2]{2,1,0:T(2,128)} %shifts_hbm.1, ...), custom_call_target="tpu_custom_call" | custom-call | tf_op jit(solution)/shard_map/pallas_call | solution.py:566
  73.8 0.0 copy-done
  73.8 1.9 %fusion = (f32[2,2,2,32,256]{4,3,2,1,0:T(8,128)}, f32[2,2,2,32,256]{4,3,2,1,0:T(8,128)}) fusion(f32[2,2,2,32,256]{4,3,2,1,0:T(8,128)} %bitcast.5, f32[2,2,2,32,256]{4,3,2,1,0:T(8,128)S(1)} %copy-done, f32[2,2,2,32,256]{4,3,2,1,0:T(8,128)} %bitcast.4), kind=kLoop, calls=%fused_computation | loop fusion | flops 131072 | bytes 1310720 | tf_op jit(solution)/shard_map/sub | solution.py:593
Async XLA Ops:
  1.3 72.5 %copy-start = (f32[2,2,2,32,256]{4,3,2,1,0:T(8,128)S(1)}, f32[2,2,2,32,256]{4,3,2,1,0:T(8,128)}, u32[]{:S(2)}) copy-start(f32[2,2,2,32,256]{4,3,2,1,0:T(8,128)} %param.17) | copy-start | bytes 786436

commit v6 on v5

--- a/solution.py
+++ b/solution.py
@@ -222,7 +222,7 @@
      mm, mb, sw, ow, alpha_ref, mix_ref, back_ref, shifts_ref, heard, load_sem, send_sem, recv_sem) = refs
     step, node, space = (lax.axis_index(a) for a in ("step", "node", "space"))
     me = step * 2 + node
-    q, chunk, half = space // 4, (space // 2) % 2, space % 2
+    q, half, chunk = (space % 16) // 2, space % 2, (space // 16 + space) % 2
 
     load_u = pltpu.make_async_copy(u_hbm, u_ref, load_sem.at[len(NAMES)])
     load_init = pltpu.make_async_copy(init_hbm, init_ref, load_sem.at[len(NAMES) + 1])
@@ -359,6 +359,9 @@
     when = (2 * (row // 16) + (row // 4) % 2).astype(jnp.float32)
     mb[0], mb[1] = parts(get("mi")[...] * (jnp.exp(rate * when) * (1.0 / STEPS)))
 
+    lax.fori_loop(1, 16, send_params, 0)
+    rp[me] = sp[...]
+
     begin = [
         jnp.where(step == 0, jnp.where(node == 0, START[m], START[2 + m]), 0.0).astype(jnp.float32) for m in range(2)
     ]
@@ -391,8 +394,6 @@
         if c == 0:
             hear(2)
             tell(3)
-    lax.fori_loop(1, 16, send_params, 0)
-    rp[me] = sp[...]
 
     for c in range(2):
         arrived(r1.at[c, 0], FIELD + c, 15)
@@ -406,7 +407,7 @@
         for h in range(2):
             def send_spec(d, _):
                 other = (q + d) % 8
-                place = 4 * other + 2 * c + h
+                place = (h + c) % 2 * 16 + 2 * other + h
                 @pl.when(place != space)
                 def _():
                     remote(s2.at[c, h, other], r2.at[space], SPACE, {"space": place}).start()
@@ -417,13 +418,14 @@
     other_u = [
         remote(u_hbm.at[pl.ds(2 * i, 2)], ub.at[node, pl.ds(2 * i, 2)], OTHER + i, {"node": 1 - node}) for i in range(2)
     ]
-    other_u[0].start()
     ub[node] = u_ref[...]
 
     arrived(rp, PARAMS, 15)
     lam = get("lam_zy")[half] + jnp.broadcast_to(get("lam_x")[2 * me + chunk][0:1], (64, 128))
     horner_tables(q, rp, coef, tab, lam)
     get("zf"), get("zt")
+    other_u[0].start()
+    other_u[1].start()
     arrived(r2, SPACE, 31)
     sw[...] = dot3((held["zf"][0], held["zf"][1]), parts(r2[...].reshape(256, 256))).reshape(4, 64, 256)
 
@@ -452,7 +454,6 @@
         return 0
 
     lax.fori_loop(1, 32, send_back, 0)
-    other_u[1].start()
     r3[chunk, half, q] = s3[space]
     get("kt")
     for c in range(2):

time: 75.9 us -> 75 us (0.988)
  Pallas kernels: 72.5 us -> 71.6 us
    pallas_call x1, Pallas kernels: 72.5 us -> 71.6 us  [on_device(): pl.pallas_call(kernel, out_shape=(block, block), in_specs=[in_any] * (6 +...]
where the time goes in v6:
time: 75 us; the launch traced here: 74.8 us
  Pallas kernels  71.6 us (95%)
  other arithmetic  1.88 us (3%)
  between operations  1.3 us (2%)
    pallas_call x1, Pallas kernels, on_device(): pl.pallas_call(kernel, out_shape=(block, block), in_specs=[in_any] * (6 +...  71.6 us
    sub x1, other arithmetic, on_device(): return (updated, rest.reshape(iterate.shape) - updated)  1.88 us

profile of v6, /device:TPU:1, one launch (start us, length us, event | category | flops | bytes accessed | tf_op | source)
XLA Modules:
  0.0 74.8 jit_solution(1179047116400662229)
XLA Ops:
  1.3 0.0 copy-start
  1.3 71.6 %shard_map.176 = (f32[4,2,32,256]{3,2,1,0:T(8,128)}, f32[4,2,32,256]{3,2,1,0:T(8,128)}) custom-call(f32[4,2,32,256]{3,2,1,0:T(8,128)} %bitcast.3, f32[2,32,256]{2,1,0:T(8,128)} %init_hbm.1, s32[1]{0:T(128)S(6)} %copy.19.alpha_hbm, f32[2,2,2,4]{3,2,1,0:T(2,128)} %mix_hbm.1, f32[2,2,2,4]{3,2,1,0:T(2,128)} %back_hbm.1, f32[2,2,2]{2,1,0:T(2,128)} %shifts_hbm.1, ...), custom_call_target="tpu_custom_call" | custom-call | tf_op jit(solution)/shard_map/pallas_call | solution.py:567
  72.9 0.0 copy-done
  72.9 1.9 %fusion = (f32[2,2,2,32,256]{4,3,2,1,0:T(8,128)}, f32[2,2,2,32,256]{4,3,2,1,0:T(8,128)}) fusion(f32[2,2,2,32,256]{4,3,2,1,0:T(8,128)} %bitcast.5, f32[2,2,2,32,256]{4,3,2,1,0:T(8,128)S(1)} %copy-done, f32[2,2,2,32,256]{4,3,2,1,0:T(8,128)} %bitcast.4), kind=kLoop, calls=%fused_computation | loop fusion | flops 131072 | bytes 1310720 | tf_op jit(solution)/shard_map/sub | solution.py:594
Async XLA Ops:
  1.3 71.6 %copy-start = (f32[2,2,2,32,256]{4,3,2,1,0:T(8,128)S(1)}, f32[2,2,2,32,256]{4,3,2,1,0:T(8,128)}, u32[]{:S(2)}) copy-start(f32[2,2,2,32,256]{4,3,2,1,0:T(8,128)} %param.17) | copy-start | bytes 786436

commit v7 on v6

--- a/solution.py
+++ b/solution.py
@@ -254,7 +254,7 @@
     def near(d):
         return {"space": (space + d) % 32}
 
-    lax.fori_loop(1, 16, greet_group, 0)
+    lax.fori_loop(1, 16, greet_group, 0, unroll=True)
     for d in (1, 31):
         pl.semaphore_signal(barrier, inc=1, device_id=near(d))
 
@@ -294,7 +294,7 @@
 
     up, down = {"space": (space + 1) % 32}, {"space": (space + 31) % 32}
     HALO_UP, HALO_DOWN, PARAMS, SPACE, W_UP, W_DOWN, BEFORE = range(7)
-    OTHER, FIELD, FORCE, BACK, CORR = 8, 10, 12, 14, 16
+    OTHER, FIELD, FORCE, BACK, CORR = 8, 10, 12, 14, 18
     pending = [
         remote(u_hbm.at[:, 1], halo.at[0], HALO_UP, up),
         remote(u_hbm.at[:, 0], halo.at[1], HALO_DOWN, down),
@@ -323,7 +323,7 @@
             remote(src.at[other], dst.at[me], sem, device).start()
             return 0
 
-        lax.fori_loop(1, 16, body, 0)
+        lax.fori_loop(1, 16, body, 0, unroll=True)
         dst[me] = src[me]
 
     def block_of(ref, count):
@@ -359,7 +359,7 @@
     when = (2 * (row // 16) + (row // 4) % 2).astype(jnp.float32)
     mb[0], mb[1] = parts(get("mi")[...] * (jnp.exp(rate * when) * (1.0 / STEPS)))
 
-    lax.fori_loop(1, 16, send_params, 0)
+    lax.fori_loop(1, 16, send_params, 0, unroll=True)
     rp[me] = sp[...]
 
     begin = [
@@ -413,7 +413,7 @@
                     remote(s2.at[c, h, other], r2.at[space], SPACE, {"space": place}).start()
                 return 0
 
-            lax.fori_loop(0, 8, send_spec, 0)
+            lax.fori_loop(0, 8, send_spec, 0, unroll=True)
     r2[space] = s2[chunk, half, q]
     other_u = [
         remote(u_hbm.at[pl.ds(2 * i, 2)], ub.at[node, pl.ds(2 * i, 2)], OTHER + i, {"node": 1 - node}) for i in range(2)
@@ -450,39 +450,48 @@
 
     def send_back(d, _):
         other = (space + d) % 32
-        remote(s3.at[other], r3.at[chunk, half, q], BACK, {"space": other}, BACK + chunk).start()
+        remote(s3.at[other], r3.at[chunk, half, q], BACK, {"space": other}, BACK + 2 * chunk + half).start()
         return 0
 
-    lax.fori_loop(1, 32, send_back, 0)
+    lax.fori_loop(1, 32, send_back, 0, unroll=True)
     r3[chunk, half, q] = s3[space]
     get("kt")
     for c in range(2):
-        for here in range(2):
-            @pl.when((chunk == c) if here else (chunk != c))
+        for h in range(2):
+            mine = (chunk == c) & (half == h)
+            turn = 2 * c + h
+
+            @pl.when(mine)
             def _():
-                part = block_of(s3, 16 - here)
-                remote(part, part, BACK, up, BACK + c).wait_recv()
-        for h in range(2):
+                part = block_of(s3, 7)
+                remote(part, part, BACK, up, BACK + turn).wait_recv()
+
+            @pl.when(jnp.logical_not(mine))
+            def _():
+                part = block_of(s3, 8)
+                remote(part, part, BACK, up, BACK + turn).wait_recv()
+
+            lanes = pl.ds(h * 128, 128)
             value = dot3((mb[0], mb[1]), parts(r3[c, h].reshape(128, 128)))
             s4[c, :, :, :, h * 128 : h * 128 + 128] = value.reshape(8, 2, 8, 128)
 
-        def send_corr(d, _):
-            other, device = group_id(d)
-            remote(s4.at[c, other // 2], r4.at[c, :, me], CORR + c, device).start()
-            return 0
-
-        lax.fori_loop(1, 16, send_corr, 0)
+            def send_corr(d, _):
+                other, device = group_id(d)
+                remote(s4.at[c, other // 2, :, :, lanes], r4.at[c, :, me, :, lanes], CORR + turn, device).start()
+                return 0
+
+            lax.fori_loop(1, 16, send_corr, 0, unroll=True)
         r4[c, :, me] = s4[c, step]
     for copy in other_u:
         copy.wait_recv()
     for c in range(2):
-        whole = r4.at[c, :, pl.ds(0, 15)]
-        remote(whole, whole, CORR + c, up).wait_recv()
+        for h in range(2):
+            whole = r4.at[c, :, pl.ds(0, 15), :, pl.ds(h * 128, 128)]
+            remote(whole, whole, CORR + 2 * c + h, up).wait_recv()
         for g in range(2):
             rows = to_sines(r4[c, g].reshape(128, 256))
             d = dot3((held["kt"][0, c], held["kt"][1, c]), rows)
             ub[g] = ub[g] + d.reshape(4, 2, 32, 256)
-    out_u[...] = ub[node] - u_ref[...]
 
     weight = [
         [jnp.where(node == 0, COLL[m][j], COLL[2 + m][j]).astype(jnp.float32) for j in range(4)] for m in range(2)
@@ -499,7 +508,6 @@
         for z in range(2):
             u = nodes_at(n, z)
             for m in range(2):
-                wb[2 * n + m, z] = sum(weight[m][j] * u[j] for j in range(4))
                 rows = [jnp.where(target[z] == 0, COLL[m][j], COLL[2 + m][j]).astype(jnp.float32) for j in range(4)]
                 wedge[z, 2 * n + m] = sum(rows[j] * u[j] for j in range(4))
     last = [
@@ -509,6 +517,12 @@
     ]
     for copy in last:
         copy.start()
+    out_u[...] = ub[node] - u_ref[...]
+    for n in range(2):
+        for z in range(2):
+            u = nodes_at(n, z)
+            for m in range(2):
+                wb[2 * n + m, z] = sum(weight[m][j] * u[j] for j in range(4))
     x = lax.broadcasted_iota(jnp.int32, (32, 256), 0)
     y = lax.broadcasted_iota(jnp.int32, (32, 256), 1)
     for n in range(2):
@@ -551,8 +565,9 @@
     for c in range(2):
         sent(su.at[c], FIELD + c, 15)
         sent(sf.at[c], FORCE + c, 15)
-        whole = r4.at[c, :, pl.ds(0, 15)]
-        remote(whole, whole, CORR + c, up).wait_send()
+        for h in range(2):
+            whole = r4.at[c, :, pl.ds(0, 15), :, pl.ds(h * 128, 128)]
+            remote(whole, whole, CORR + 2 * c + h, up).wait_send()
     sent(rp, PARAMS, 15)
     sent(r2, SPACE, 31)
     sent(s3, BACK, 31)
@@ -585,7 +600,7 @@
         + [vmem(4, 64, 256)] * 2
         + [pltpu.SMEM((1,), jnp.int32), pltpu.SMEM((2, 2, 2, 4), f32), pltpu.SMEM((2, 2, 2, 4), f32), pltpu.SMEM((2, 2, 2), f32)]
         + [pltpu.SemaphoreType.REGULAR((4,))]
-        + [pltpu.SemaphoreType.DMA((len(NAMES) + 6,)), pltpu.SemaphoreType.DMA((18,)), pltpu.SemaphoreType.DMA((18,))],
+        + [pltpu.SemaphoreType.DMA((len(NAMES) + 6,)), pltpu.SemaphoreType.DMA((22,)), pltpu.SemaphoreType.DMA((22,))],
         compiler_params=pltpu.CompilerParams(
             collective_id=0, has_side_effects=True, vmem_limit_bytes=63 * 1024 * 1024
         ),

time: 75 us -> 74.1 us (0.988)
  Pallas kernels: 71.6 us -> 70.7 us
    pallas_call x1, Pallas kernels: 71.6 us -> 70.7 us  [on_device(): pl.pallas_call(kernel, out_shape=(block, block), in_specs=[in_any] * (6 +...]
where the time goes in v7:
time: 74.1 us; the launch traced here: 73.9 us
  Pallas kernels  70.7 us (95%)
  other arithmetic  1.88 us (3%)
  between operations  1.3 us (2%)
    pallas_call x1, Pallas kernels, on_device(): pl.pallas_call(kernel, out_shape=(block, block), in_specs=[in_any] * (6 +...  70.7 us
    sub x1, other arithmetic, on_device(): return (updated, rest.reshape(iterate.shape) - updated)  1.88 us

profile of v7, /device:TPU:1, one launch (start us, length us, event | category | flops | bytes accessed | tf_op | source)
XLA Modules:
  0.0 73.9 jit_solution(10823092432197251498)
XLA Ops:
  1.3 0.0 copy-start
  1.3 70.7 %shard_map.176 = (f32[4,2,32,256]{3,2,1,0:T(8,128)}, f32[4,2,32,256]{3,2,1,0:T(8,128)}) custom-call(f32[4,2,32,256]{3,2,1,0:T(8,128)} %bitcast.3, f32[2,32,256]{2,1,0:T(8,128)} %init_hbm.1, s32[1]{0:T(128)S(6)} %copy.19.alpha_hbm, f32[2,2,2,4]{3,2,1,0:T(2,128)} %mix_hbm.1, f32[2,2,2,4]{3,2,1,0:T(2,128)} %back_hbm.1, f32[2,2,2]{2,1,0:T(2,128)} %shifts_hbm.1, ...), custom_call_target="tpu_custom_call" | custom-call | tf_op jit(solution)/shard_map/pallas_call | solution.py:582
  72.0 0.0 copy-done
  72.0 1.9 %fusion = (f32[2,2,2,32,256]{4,3,2,1,0:T(8,128)}, f32[2,2,2,32,256]{4,3,2,1,0:T(8,128)}) fusion(f32[2,2,2,32,256]{4,3,2,1,0:T(8,128)} %bitcast.5, f32[2,2,2,32,256]{4,3,2,1,0:T(8,128)S(1)} %copy-done, f32[2,2,2,32,256]{4,3,2,1,0:T(8,128)} %bitcast.4), kind=kLoop, calls=%fused_computation | loop fusion | flops 131072 | bytes 1310720 | tf_op jit(solution)/shard_map/sub | solution.py:609
Async XLA Ops:
  1.3 70.7 %copy-start = (f32[2,2,2,32,256]{4,3,2,1,0:T(8,128)S(1)}, f32[2,2,2,32,256]{4,3,2,1,0:T(8,128)}, u32[]{:S(2)}) copy-start(f32[2,2,2,32,256]{4,3,2,1,0:T(8,128)} %param.17) | copy-start | bytes 786436
